TPU v7x, 32 devices: a whole 2x2x4 slice. The times are simulated.
32 devices in a mesh: seq: 8 (over z, y), ch: 4 (over x, core).
Axes of the slice: x: 2, y: 2, z: 4, core: 2. Of those that a mesh axis runs over, the one named last changes fastest.
Arguments:
- query_proj: bfloat16 [4096, 512], P('seq', 'ch'), may hold values from -6 to 6
- key_proj: bfloat16 [4096, 512], P('seq', 'ch'), may hold values from -6 to 6
- value_proj: bfloat16 [4096, 512], P('seq', 'ch'), may hold values from -6 to 6
- filter_taps: float32 [4096, 128], P('seq'), may hold values from -1.1 to 1.1, as said below
- skip_gain: float32 [512], P('ch'), may hold values from 0.3 to 3
- grad_mixer: bfloat16 [4096, 512], P('seq', 'ch'), may hold values from -6 to 6
Outputs:
- mixer_out: bfloat16 [4096, 512], P('seq', 'ch')
- grad_query: bfloat16 [4096, 512], P('seq', 'ch')
- grad_key: bfloat16 [4096, 512], P('seq', 'ch')
- grad_value: bfloat16 [4096, 512], P('seq', 'ch')
- grad_filter: float32 [4096, 128], P('seq', 'ch')
Inputs may be any that keep to these rules, and one draw needn't show every extreme that they name: `filter_taps`: real-valued filter taps.
All inputs are finite; a program needn't handle non-finite values.
Results may differ from a plain program's by a relative error of at most 0.001.
Values sent between devices are 32-bit elements; how exact they have to be, the bound alone decides.
A program may use at most 64 MiB of HBM per device.

v0:
```python
import math

import jax
import jax.numpy as jnp
from jax import lax
from jax.sharding import PartitionSpec as P

HIGHEST = lax.Precision.HIGHEST


def from_partner(array, axis, distance):
    return lax.ppermute(array, axis, [(i, i ^ 1 << distance) for i in range(lax.axis_size(axis))])


def complex_mul(left_real, left_imag, right_real, right_imag):
    return (
        left_real * right_real - left_imag * right_imag,
        left_real * right_imag + left_imag * right_real,
    )


def reverse_bits(value, sections):
    result = value * 0
    for section in range(sections):
        result = result + value // 2**section % 2 * 2 ** (sections - 1 - section)
    return result


def apply_table(form, table_real, table_imag, data_real, data_imag):
    first = jnp.einsum(form, table_real, data_real, precision=HIGHEST) - jnp.einsum(
        form, table_imag, data_imag, precision=HIGHEST
    )
    second = jnp.einsum(form, table_real, data_imag, precision=HIGHEST) + jnp.einsum(
        form, table_imag, data_real, precision=HIGHEST
    )
    return (first, second)


def local_table(count, sign):
    index = jnp.arange(count, dtype=jnp.int32)
    angles = (
        sign * 2.0 * math.pi / count * (index[:, None] * index[None, :] % count).astype(jnp.float32)
    )
    return (jnp.cos(angles), jnp.sin(angles))


def seq_twiddle(local_rows, seq_total, freq_index, sign):
    index = jnp.arange(local_rows, dtype=jnp.int32)
    angles = sign * 2.0 * math.pi / seq_total * (index * freq_index).astype(jnp.float32)
    return (jnp.cos(angles)[None, :, None], jnp.sin(angles)[None, :, None])


def cross_forward(real_part, imag_part, seq_count, own_index):
    sections = seq_count.bit_length() - 1
    for section in reversed(range(sections)):
        block_span = 2 ** (section + 1)
        half_span = 2**section
        offset = own_index % block_span
        is_upper = offset >= half_span
        angle = -2.0 * math.pi / block_span * (offset - half_span).astype(jnp.float32)
        partner_real, partner_imag = from_partner((real_part, imag_part), "seq", section)
        diff_real, diff_imag = complex_mul(
            partner_real - real_part, partner_imag - imag_part, jnp.cos(angle), jnp.sin(angle)
        )
        real_part = jnp.where(is_upper, diff_real, real_part + partner_real)
        imag_part = jnp.where(is_upper, diff_imag, imag_part + partner_imag)
    return (real_part, imag_part)


def cross_inverse(real_part, imag_part, seq_count, own_index):
    sections = seq_count.bit_length() - 1
    for section in range(sections):
        block_span = 2 ** (section + 1)
        half_span = 2**section
        offset = own_index % block_span
        is_upper = offset >= half_span
        paired = jnp.where(is_upper, offset - half_span, offset)
        angle = 2.0 * math.pi / block_span * paired.astype(jnp.float32)
        conj_real = jnp.cos(angle)
        conj_imag = jnp.sin(angle)
        partner_real, partner_imag = from_partner((real_part, imag_part), "seq", section)
        turned_partner = complex_mul(partner_real, partner_imag, conj_real, conj_imag)
        turned_own = complex_mul(real_part, imag_part, conj_real, conj_imag)
        lower_real = 0.5 * (real_part + turned_partner[0])
        lower_imag = 0.5 * (imag_part + turned_partner[1])
        upper_real = 0.5 * (partner_real - turned_own[0])
        upper_imag = 0.5 * (partner_imag - turned_own[1])
        real_part = jnp.where(is_upper, upper_real, lower_real)
        imag_part = jnp.where(is_upper, upper_imag, lower_imag)
    return (real_part, imag_part)


def forward_transform(real_part, imag_part, seq_count, own_index):
    sections = seq_count.bit_length() - 1
    real_part, imag_part = cross_forward(real_part, imag_part, seq_count, own_index)
    local_rows = real_part.shape[1]
    freq_index = reverse_bits(own_index, sections)
    twist_real, twist_imag = seq_twiddle(local_rows, local_rows * seq_count, freq_index, -1.0)
    real_part, imag_part = complex_mul(real_part, imag_part, twist_real, twist_imag)
    table_real, table_imag = local_table(local_rows, -1.0)
    return apply_table("kj,ajw->akw", table_real, table_imag, real_part, imag_part)


def inverse_transform(real_part, imag_part, seq_count, own_index):
    sections = seq_count.bit_length() - 1
    local_rows = real_part.shape[1]
    table_real, table_imag = local_table(local_rows, 1.0)
    factor = 1.0 / local_rows
    real_part, imag_part = apply_table(
        "jk,akw->ajw", table_real * factor, table_imag * factor, real_part, imag_part
    )
    freq_index = reverse_bits(own_index, sections)
    twist_real, twist_imag = seq_twiddle(local_rows, local_rows * seq_count, freq_index, 1.0)
    real_part, imag_part = complex_mul(real_part, imag_part, twist_real, twist_imag)
    return cross_inverse(real_part, imag_part, seq_count, own_index)


def local(query_proj, key_proj, value_proj, filter_taps, skip_gain, grad_mixer):
    seq_count = lax.axis_size("seq")
    own_index = lax.axis_index("seq")
    local_rows, local_ch = query_proj.shape
    filters = filter_taps.shape[1]
    repeats = local_ch // filters
    seq_total = local_rows * seq_count
    query = query_proj.astype(jnp.float32)
    key_data = key_proj.astype(jnp.float32)
    value_data = value_proj.astype(jnp.float32)
    upstream = grad_mixer.astype(jnp.float32)
    mixed = key_data * value_data
    grad_in = upstream * query
    signals = jnp.concatenate([filter_taps, mixed, grad_in], axis=1)
    positions = own_index * local_rows + jnp.arange(local_rows, dtype=jnp.int32)
    theta = math.pi / seq_total * positions.astype(jnp.float32)
    cos_theta = jnp.cos(theta)[:, None]
    sin_theta = jnp.sin(theta)[:, None]
    start_real = jnp.stack([signals, signals * cos_theta])
    start_imag = jnp.stack([jnp.zeros_like(signals), -signals * sin_theta])
    spec_real, spec_imag = forward_transform(start_real, start_imag, seq_count, own_index)
    taps_real = jnp.tile(spec_real[:, :, :filters], (1, 1, repeats))
    taps_imag = jnp.tile(spec_imag[:, :, :filters], (1, 1, repeats))
    mixed_real = spec_real[:, :, filters : filters + local_ch]
    mixed_imag = spec_imag[:, :, filters : filters + local_ch]
    grads_real = spec_real[:, :, filters + local_ch :]
    grads_imag = spec_imag[:, :, filters + local_ch :]
    conv_real, conv_imag = complex_mul(taps_real, taps_imag, mixed_real, mixed_imag)
    back_real, back_imag = complex_mul(taps_real, -taps_imag, grads_real, grads_imag)
    corr_real, corr_imag = complex_mul(mixed_real, -mixed_imag, grads_real, grads_imag)
    corr_real = corr_real.reshape(2, local_rows, repeats, filters).sum(axis=2)
    corr_imag = corr_imag.reshape(2, local_rows, repeats, filters).sum(axis=2)
    scale = 1.0 / math.sqrt(seq_total)
    filt_real, filt_imag = (corr_real, corr_imag)
    out_real, out_imag = inverse_transform(
        jnp.concatenate([conv_real, back_real, filt_real], axis=2),
        jnp.concatenate([conv_imag, back_imag, filt_imag], axis=2),
        seq_count,
        own_index,
    )
    real_field = 0.5 * (out_real[0] + cos_theta * out_real[1] - sin_theta * out_imag[1])
    imag_field = 0.5 * (out_imag[0] + sin_theta * out_real[1] + cos_theta * out_imag[1])
    real_field, imag_field = (real_field, imag_field)
    conv = real_field[:, :local_ch]
    back_corr = real_field[:, local_ch : 2 * local_ch]
    filt_field = real_field[:, 2 * local_ch :]
    grad_filter = lax.psum_scatter(filt_field, "ch", scatter_dimension=1, tiled=True) * scale
    gain_row = skip_gain[None, :]
    pre = conv + gain_row * mixed
    mixer_out = (query * pre).astype(jnp.bfloat16)
    grad_query = (upstream * pre).astype(jnp.bfloat16)
    back = back_corr + gain_row * grad_in
    grad_key = (back * value_data).astype(jnp.bfloat16)
    grad_value = (back * key_data).astype(jnp.bfloat16)
    return (mixer_out, grad_query, grad_key, grad_value, grad_filter)


def solution(mesh):
    in_specs = (
        P("seq", "ch"),
        P("seq", "ch"),
        P("seq", "ch"),
        P("seq", None),
        P("ch"),
        P("seq", "ch"),
    )
    out_specs = (P("seq", "ch"), P("seq", "ch"), P("seq", "ch"), P("seq", "ch"), P("seq", "ch"))
    return jax.shard_map(local, mesh=mesh, in_specs=in_specs, out_specs=out_specs, check_vma=False)
```

profile of v0, /device:TPU:25, one launch (start us, length us, event | category | flops | bytes accessed | tf_op | source)
XLA Modules:
  0.0 672.2 jit_solution(12233482904716981556)
XLA Ops:
  7.2 0.0 reduce-scatter.2.cloned.1.call-start
  7.2 1.0 copy.11
  8.2 1.0 copy.12
  9.2 1.0 copy.13
  10.3 1.0 copy.14
  11.3 0.0 copy-start.5
  11.3 1.1 copy.15
  12.4 0.1 convert_multiply_fusion.1
  12.6 0.1 maximum_bitcast_fusion
  12.6 0.2 fusion.30
  12.9 1.3 pad_maximum_fusion
  14.2 0.1 collective-permute-start
  14.2 1.4 stack.13
  15.6 2.3 collective-permute-start.1
  18.1 100.9 %collective-permute-done = f32[2,512,384]{1,2,0:T(8,128)} collective-permute-done((f32[2,512,384]{1,2,0:T(8,128)}, f32[2,512,384]{1,2,0:T(8,128)}, u32[]{:S(2)}, u32[]{:S(2)}) %collective-permute-start) | collective-permute-done | bytes 1572896 | tf_op jit(solution)/shard_map/ppermute | solution.py:12
  119.0 33.7 %collective-permute-done.1 = f32[2,512,384]{1,2,0:T(8,128)} collective-permute-done((f32[2,512,384]{1,2,0:T(8,128)}, f32[2,512,384]{1,2,0:T(8,128)}, u32[]{:S(2)}, u32[]{:S(2)}) %collective-permute-start.1) | collective-permute-done | bytes 1572896 | tf_op jit(solution)/shard_map/ppermute | solution.py:12
  152.7 4.3 add_select_fusion.6
  157.0 0.0 collective-permute-start.2
  157.0 1.5 collective-permute-start.3
  158.6 34.1 %collective-permute-done.2 = f32[2,512,384]{1,2,0:T(8,128)S(1)} collective-permute-done((f32[2,512,384]{1,2,0:T(8,128)}, f32[2,512,384]{1,2,0:T(8,128)S(1)}, u32[]{:S(2)}, u32[]{:S(2)}) %collective-permute-start.2) | collective-permute-done | bytes 1572896 | tf_op jit(solution)/shard_map/ppermute | solution.py:12
  192.7 1.2 copy-done.2
  193.8 32.6 %collective-permute-done.3 = f32[2,512,384]{1,2,0:T(8,128)} collective-permute-done((f32[2,512,384]{1,2,0:T(8,128)}, f32[2,512,384]{1,2,0:T(8,128)}, u32[]{:S(2)}, u32[]{:S(2)}) %collective-permute-start.3) | collective-permute-done | bytes 1572896 | tf_op jit(solution)/shard_map/ppermute | solution.py:12
  226.5 3.9 add_select_fusion.4
  230.3 1.3 collective-permute-start.4
  231.7 0.2 collective-permute-start.5
  232.2 32.9 %collective-permute-done.4 = f32[2,512,384]{1,2,0:T(8,128)} collective-permute-done((f32[2,512,384]{1,2,0:T(8,128)S(1)}, f32[2,512,384]{1,2,0:T(8,128)}, u32[]{:S(2)}, u32[]{:S(2)}) %collective-permute-start.4) | collective-permute-done | bytes 1572896 | tf_op jit(solution)/shard_map/ppermute | solution.py:12
  265.1 33.7 %collective-permute-done.5 = f32[2,512,384]{1,2,0:T(8,128)} collective-permute-done((f32[2,512,384]{1,2,0:T(8,128)S(1)}, f32[2,512,384]{1,2,0:T(8,128)}, u32[]{:S(2)}, u32[]{:S(2)}) %collective-permute-start.5) | collective-permute-done | bytes 1572896 | tf_op jit(solution)/shard_map/ppermute | solution.py:12
  298.8 2.7 add_select_fusion.2
  301.5 6.7 fusion.10
  308.1 6.8 %fusion.8 = f32[2,384,512]{2,1,0:T(8,128)S(1)} fusion(f32[2,512,384]{1,2,0:T(8,128)S(1)} %get-tuple-element.15, f32[2,512,384]{1,2,0:T(8,128)S(1)} %get-tuple-element.14, f32[512]{0:T(512)S(1)} %get-tuple-element.43, f32[512]{0:T(512)S(1)} %get-tuple-element.44), kind=kOutput, calls=%fused_computation.33 | convolution fusion | flops 2420768768 | bytes 4722688 | tf_op jit(solution)/shard_map/kj,ajw->akw/dot_general | solution.py:33
  315.0 6.6 subtract_bitcast_fusion.1
  321.6 6.9 %add_bitcast_fusion.1 = f32[2,512,384]{1,2,0:T(8,128)S(1)} fusion(f32[2,384,512]{2,1,0:T(8,128)S(1)} %fusion.8, f32[2,512,384]{1,2,0:T(8,128)S(1)} %get-tuple-element.15, f32[2,512,384]{1,2,0:T(8,128)S(1)} %get-tuple-element.14, f32[512]{0:T(512)S(1)} %get-tuple-element.43, f32[512]{0:T(512)S(1)} %get-tuple-element.44), kind=kOutput, calls=%fused_computation.10 | convolution fusion | flops 2421161984 | bytes 6295552 | tf_op jit(solution)/shard_map/kj,ajw->akw/dot_general | solution.py:33
  328.5 0.4 multiply_subtract_fusion.2
  328.9 0.6 multiply_subtract_fusion.3
  329.4 7.0 %fusion.1 = f32[2,384,512]{2,1,0:T(8,128)S(1)} fusion(f32[2,512,128]{1,2,0:T(8,128)S(1)} %get-tuple-element.23, f32[2,512,128]{1,2,0:T(8,128)S(1)} %get-tuple-element.26, f32[2,512,128]{1,2,0:T(8,128)S(1)} %get-tuple-element.22), kind=kOutput, calls=%fused_computation.26 | convolution fusion | flops 2420637696 | bytes 3145728 | tf_op jit(solution)/shard_map/jk,akw->ajw/dot_general | solution.py:30
  336.4 6.5 fusion
  342.9 6.7 %convolution_add_fusion = f32[2,384,512]{2,1,0:T(8,128)S(1)} fusion(f32[2,384,512]{2,1,0:T(8,128)S(1)} %fusion, f32[2,512,128]{1,2,0:T(8,128)S(1)} %get-tuple-element.23, f32[2,512,128]{1,2,0:T(8,128)S(1)} %get-tuple-element.26, f32[2,512,128]{1,2,0:T(8,128)S(1)} %get-tuple-element.22), kind=kOutput, calls=%fused_computation.23 | convolution fusion | flops 2421030912 | bytes 4718592 | tf_op jit(solution)/shard_map/jk,akw->ajw/dot_general | solution.py:33
  349.7 6.9 %add_bitcast_fusion = (f32[2,512,384]{1,2,0:T(8,128)S(1)}, f32[2,512,384]{1,2,0:T(8,128)S(1)}) fusion(f32[2,384,512]{2,1,0:T(8,128)S(1)} %convolution_add_fusion, f32[512]{0:T(512)S(1)} %get-tuple-element.45, f32[512]{0:T(512)S(1)} %get-tuple-element.46, f32[2,384,512]{2,1,0:T(8,128)S(1)} %fusion.1, f32[2,512,128]{1,2,0:T(8,128)S(1)} %get-tuple-element.25, ...), kind=kOutput, calls=%fused_computation.8 | convolution fusion | flops 2423390208 | bytes 7868416 | tf_op jit(solution)/shard_map/jk,akw->ajw/dot_general | solution.py:30
  356.6 1.3 collective-permute-start.6
  357.9 0.2 collective-permute-start.7
  358.3 32.1 %collective-permute-done.6 = f32[2,512,384]{1,2,0:T(8,128)} collective-permute-done((f32[2,512,384]{1,2,0:T(8,128)S(1)}, f32[2,512,384]{1,2,0:T(8,128)}, u32[]{:S(2)}, u32[]{:S(2)}) %collective-permute-start.6) | collective-permute-done | bytes 1572896 | tf_op jit(solution)/shard_map/ppermute | solution.py:12
  390.4 33.7 %collective-permute-done.7 = f32[2,512,384]{1,2,0:T(8,128)} collective-permute-done((f32[2,512,384]{1,2,0:T(8,128)S(1)}, f32[2,512,384]{1,2,0:T(8,128)}, u32[]{:S(2)}, u32[]{:S(2)}) %collective-permute-start.7) | collective-permute-done | bytes 1572896 | tf_op jit(solution)/shard_map/ppermute | solution.py:12
  424.1 4.0 multiply_select_fusion.3
  428.1 1.0 collective-permute-start.8
  429.1 0.5 collective-permute-start.9
  429.7 31.2 %collective-permute-done.8 = f32[2,512,384]{1,2,0:T(8,128)} collective-permute-done((f32[2,512,384]{1,2,0:T(8,128)S(1)}, f32[2,512,384]{1,2,0:T(8,128)}, u32[]{:S(2)}, u32[]{:S(2)}) %collective-permute-start.8) | collective-permute-done | bytes 1572896 | tf_op jit(solution)/shard_map/ppermute | solution.py:12
  460.9 33.7 %collective-permute-done.9 = f32[2,512,384]{1,2,0:T(8,128)} collective-permute-done((f32[2,512,384]{1,2,0:T(8,128)S(1)}, f32[2,512,384]{1,2,0:T(8,128)}, u32[]{:S(2)}, u32[]{:S(2)}) %collective-permute-start.9) | collective-permute-done | bytes 1572896 | tf_op jit(solution)/shard_map/ppermute | solution.py:12
  494.6 4.0 multiply_select_fusion.1
  498.6 0.1 collective-permute-start.10
  498.7 2.4 collective-permute-start.11
  501.2 101.2 %collective-permute-done.10 = f32[2,512,384]{1,2,0:T(8,128)} collective-permute-done((f32[2,512,384]{1,2,0:T(8,128)S(1)}, f32[2,512,384]{1,2,0:T(8,128)}, u32[]{:S(2)}, u32[]{:S(2)}) %collective-permute-start.10) | collective-permute-done | bytes 1572896 | tf_op jit(solution)/shard_map/ppermute | solution.py:12
  602.4 33.7 %collective-permute-done.11 = f32[2,512,384]{1,2,0:T(8,128)} collective-permute-done((f32[2,512,384]{1,2,0:T(8,128)S(1)}, f32[2,512,384]{1,2,0:T(8,128)}, u32[]{:S(2)}, u32[]{:S(2)}) %collective-permute-start.11) | collective-permute-done | bytes 1572896 | tf_op jit(solution)/shard_map/ppermute | solution.py:12
  636.1 2.7 multiply_select_fusion
  638.7 0.0 copy-start.6
  638.7 0.0 copy-start.7
  638.8 2.0 fusion.24
  640.8 0.9 fusion.52
  641.7 0.0 reduce-scatter.2.cloned.1.call-update
  641.7 0.8 copy.17
  642.5 0.8 copy.18
  643.2 0.8 copy.19
  644.0 0.8 copy.20
  644.7 18.9 %reduce-scatter.2.cloned.1.call-done = f32[512,32]{0,1:T(8,128)} async-done(((f32[512,128]{0,1:T(8,128)}), f32[512,32]{0,1:T(8,128)}) %reduce-scatter.2.cloned.1.call-update) | async-done | bytes 65552 | tf_op jit(solution)/shard_map/reduce_scatter | solution.py:164
  663.7 1.5 broadcast_multiply_fusion
  (15 shorter events, 0.2 us)
Async XLA Ops:
  7.2 656.5 %reduce-scatter.2.cloned.1.call-start = ((), (), s32[]{:S(2)}) async-start(), calls=%async_computation.1 | async-start | bytes 327680 | tf_op jit(solution)/shard_map/reduce_scatter | solution.py:164
  11.3 1.4 copy-start.5
  14.2 104.8 %collective-permute-start = (f32[2,512,384]{1,2,0:T(8,128)}, f32[2,512,384]{1,2,0:T(8,128)}, u32[]{:S(2)}, u32[]{:S(2)}) collective-permute-start(f32[2,512,384]{1,2,0:T(8,128)} %pad_maximum_fusion), channel_id=1, source_target_pairs={{0,16},{4,20},{8,24},{12,28},{16,0},{20,4},{24,8},{28,12},{1,17},{... | collective-permute-start | bytes 4718600 | tf_op jit(solution)/shard_map/ppermute | solution.py:12
  15.6 137.1 %collective-permute-start.1 = (f32[2,512,384]{1,2,0:T(8,128)}, f32[2,512,384]{1,2,0:T(8,128)}, u32[]{:S(2)}, u32[]{:S(2)}) collective-permute-start(f32[2,512,384]{1,2,0:T(8,128)} %stack.13), channel_id=1, source_target_pairs={{0,16},{4,20},{8,24},{12,28},{16,0},{20,4},{24,8},{28,12},{1,17},{... | collective-permute-start | bytes 4718600 | tf_op jit(solution)/shard_map/ppermute | solution.py:12
  157.0 35.7 %collective-permute-start.2 = (f32[2,512,384]{1,2,0:T(8,128)}, f32[2,512,384]{1,2,0:T(8,128)S(1)}, u32[]{:S(2)}, u32[]{:S(2)}) collective-permute-start(f32[2,512,384]{1,2,0:T(8,128)} %get-tuple-element.18), channel_id=1, source_target_pairs={{0,8},{4,12},{8,0},{12,4},{16,24},{20,28},{24,16},{28,20},{1,9},{5... | collective-permute-start | bytes 4718600 | tf_op jit(solution)/shard_map/ppermute | solution.py:12
  157.0 69.5 %collective-permute-start.3 = (f32[2,512,384]{1,2,0:T(8,128)}, f32[2,512,384]{1,2,0:T(8,128)}, u32[]{:S(2)}, u32[]{:S(2)}) collective-permute-start(f32[2,512,384]{1,2,0:T(8,128)} %get-tuple-element.19), channel_id=1, source_target_pairs={{0,8},{4,12},{8,0},{12,4},{16,24},{20,28},{24,16},{28,20},{1,9},{5... | collective-permute-start | bytes 4718600 | tf_op jit(solution)/shard_map/ppermute | solution.py:12
  192.7 1.2 copy-start.2
  230.3 34.7 %collective-permute-start.4 = (f32[2,512,384]{1,2,0:T(8,128)S(1)}, f32[2,512,384]{1,2,0:T(8,128)}, u32[]{:S(2)}, u32[]{:S(2)}) collective-permute-start(f32[2,512,384]{1,2,0:T(8,128)S(1)} %get-tuple-element.16), channel_id=1, source_target_pairs={{0,4},{4,0},{8,12},{12,8},{16,20},{20,16},{24,28},{28,24},{1,5},{5... | collective-permute-start | bytes 4718600 | tf_op jit(solution)/shard_map/ppermute | solution.py:12
  231.7 67.1 %collective-permute-start.5 = (f32[2,512,384]{1,2,0:T(8,128)S(1)}, f32[2,512,384]{1,2,0:T(8,128)}, u32[]{:S(2)}, u32[]{:S(2)}) collective-permute-start(f32[2,512,384]{1,2,0:T(8,128)S(1)} %get-tuple-element.17), channel_id=1, source_target_pairs={{0,4},{4,0},{8,12},{12,8},{16,20},{20,16},{24,28},{28,24},{1,5},{5... | collective-permute-start | bytes 4718600 | tf_op jit(solution)/shard_map/ppermute | solution.py:12
  356.6 33.8 %copy-start.3 = (f32[2,512,384]{1,2,0:T(8,128)}, f32[2,512,384]{1,2,0:T(8,128)S(1)}, u32[]{:S(2)}) copy-start(f32[2,512,384]{1,2,0:T(8,128)S(1)} %get-tuple-element.20) | copy-start | bytes 4718596
  356.6 33.8 %copy-start.4 = (f32[2,512,384]{1,2,0:T(8,128)}, f32[2,512,384]{1,2,0:T(8,128)S(1)}, u32[]{:S(2)}) copy-start(f32[2,512,384]{1,2,0:T(8,128)S(1)} %get-tuple-element.21) | copy-start | bytes 4718596
  356.6 33.8 %collective-permute-start.6 = (f32[2,512,384]{1,2,0:T(8,128)S(1)}, f32[2,512,384]{1,2,0:T(8,128)}, u32[]{:S(2)}, u32[]{:S(2)}) collective-permute-start(f32[2,512,384]{1,2,0:T(8,128)S(1)} %get-tuple-element.21), channel_id=1, source_target_pairs={{0,4},{4,0},{8,12},{12,8},{16,20},{20,16},{24,28},{28,24},{1,5},{5... | collective-permute-start | bytes 4718600 | tf_op jit(solution)/shard_map/ppermute | solution.py:12
  357.9 66.2 %collective-permute-start.7 = (f32[2,512,384]{1,2,0:T(8,128)S(1)}, f32[2,512,384]{1,2,0:T(8,128)}, u32[]{:S(2)}, u32[]{:S(2)}) collective-permute-start(f32[2,512,384]{1,2,0:T(8,128)S(1)} %get-tuple-element.20), channel_id=1, source_target_pairs={{0,4},{4,0},{8,12},{12,8},{16,20},{20,16},{24,28},{28,24},{1,5},{5... | collective-permute-start | bytes 4718600 | tf_op jit(solution)/shard_map/ppermute | solution.py:12
  428.0 32.9 %copy-start = (f32[2,512,384]{1,2,0:T(8,128)}, f32[2,512,384]{1,2,0:T(8,128)S(1)}, u32[]{:S(2)}) copy-start(f32[2,512,384]{1,2,0:T(8,128)S(1)} %get-tuple-element.12) | copy-start | bytes 4718596
  428.0 32.9 %copy-start.1 = (f32[2,512,384]{1,2,0:T(8,128)}, f32[2,512,384]{1,2,0:T(8,128)S(1)}, u32[]{:S(2)}) copy-start(f32[2,512,384]{1,2,0:T(8,128)S(1)} %get-tuple-element.13) | copy-start | bytes 4718596
  428.1 32.9 %collective-permute-start.8 = (f32[2,512,384]{1,2,0:T(8,128)S(1)}, f32[2,512,384]{1,2,0:T(8,128)}, u32[]{:S(2)}, u32[]{:S(2)}) collective-permute-start(f32[2,512,384]{1,2,0:T(8,128)S(1)} %get-tuple-element.13), channel_id=1, source_target_pairs={{0,8},{4,12},{8,0},{12,4},{16,24},{20,28},{24,16},{28,20},{1,9},{5... | collective-permute-start | bytes 4718600 | tf_op jit(solution)/shard_map/ppermute | solution.py:12
  429.1 65.6 %collective-permute-start.9 = (f32[2,512,384]{1,2,0:T(8,128)S(1)}, f32[2,512,384]{1,2,0:T(8,128)}, u32[]{:S(2)}, u32[]{:S(2)}) collective-permute-start(f32[2,512,384]{1,2,0:T(8,128)S(1)} %get-tuple-element.12), channel_id=1, source_target_pairs={{0,8},{4,12},{8,0},{12,4},{16,24},{20,28},{24,16},{28,20},{1,9},{5... | collective-permute-start | bytes 4718600 | tf_op jit(solution)/shard_map/ppermute | solution.py:12
  498.6 103.8 %collective-permute-start.10 = (f32[2,512,384]{1,2,0:T(8,128)S(1)}, f32[2,512,384]{1,2,0:T(8,128)}, u32[]{:S(2)}, u32[]{:S(2)}) collective-permute-start(f32[2,512,384]{1,2,0:T(8,128)S(1)} %get-tuple-element.11), channel_id=1, source_target_pairs={{0,16},{4,20},{8,24},{12,28},{16,0},{20,4},{24,8},{28,12},{1,17},{... | collective-permute-start | bytes 4718600 | tf_op jit(solution)/shard_map/ppermute | solution.py:12
  498.7 137.4 %collective-permute-start.11 = (f32[2,512,384]{1,2,0:T(8,128)S(1)}, f32[2,512,384]{1,2,0:T(8,128)}, u32[]{:S(2)}, u32[]{:S(2)}) collective-permute-start(f32[2,512,384]{1,2,0:T(8,128)S(1)} %get-tuple-element.10), channel_id=1, source_target_pairs={{0,16},{4,20},{8,24},{12,28},{16,0},{20,4},{24,8},{28,12},{1,17},{... | collective-permute-start | bytes 4718600 | tf_op jit(solution)/shard_map/ppermute | solution.py:12
  638.7 2.1 copy-start.6
  638.7 2.0 copy-start.7
Sparse Core Ops, SparseCore 0:
  641.8 21.7 reduce-scatter.1
where the time goes:
time: 683 us; the launch traced here: 672 us
  waiting for transfers between devices  552 us (81%)
  matrix products  54.1 us (8%)
  other arithmetic  28.5 us (4%)
  between operations  15.5 us (2%)
  starting transfers between devices  10.9 us (2%)
  local copies, waits for them, and re-layouts  10.8 us (2%)
    ppermute x12, waiting for transfers between devices, from_partner(): lax.ppermute(array, axis, [(i, i ^ 1 << distance) for i in range(lax.axis...  533 us
    reduce_scatter x1, waiting for transfers between devices, local(): lax.psum_scatter(filt_field, 'ch', scatter_dimension=1, tiled=True) * scale  18.9 us
  transfers between devices with their start and end apart: 13, of which 13 were waited for; matrix products, arithmetic and copies ran while one was open for 1% of the time, Pallas kernels for 0%

commit v1 on v0

v1 whole, which is shorter than its diff:
```python
import functools
import math

import jax
import jax.numpy as jnp
import ml_dtypes
import numpy as np
from jax import lax
from jax.experimental import pallas as pl
from jax.experimental.pallas import tpu as pltpu
from jax.sharding import PartitionSpec as P

MESH = pl.DeviceIdType.MESH
LANES = 128


def halves(table):
    head = table.astype(np.float32).astype(ml_dtypes.bfloat16)
    tail = (table - head.astype(np.float64)).astype(np.float32).astype(ml_dtypes.bfloat16)
    return np.stack([head, tail])


@functools.lru_cache(maxsize=4)
def tables(seq_count, ch_count, nb, filters):
    ndev = seq_count * ch_count
    nf = filters // ndev
    dup = max(1, 8 // (nb * nf))
    n1 = seq_count * nb
    total = n1 * LANES
    a = np.arange(n1)
    ang = 2 * np.pi / n1 * ((a[:, None] + 0.25) * a[None, :])
    stack = np.concatenate([np.cos(ang), -np.sin(ang)], 0)
    first = np.kron(stack, np.eye(2 * nf))
    pick = np.kron(np.array([[1.0], [1.0]]), np.kron(np.eye(dup)[:1], np.eye(nf)))
    first_taps = np.kron(stack, pick)
    last = first.T / total
    keep = np.kron(np.ones((dup, 1)), np.concatenate([np.eye(nf), np.zeros((nf, nf))], 1))
    last_filt = np.kron(stack.T, keep) / total / math.sqrt(total)
    b = np.arange(LANES)
    turn = 2 * np.pi / total * ((a[:, None] + 0.25) * b[None, :])
    twist = np.repeat(np.stack([np.cos(turn), -np.sin(turn)]), 2 * nf, axis=1)
    ang2 = 2 * np.pi / LANES * (b[:, None] * b[None, :] % LANES)
    fr, fi = np.cos(ang2), -np.sin(ang2)
    second = np.block([[fr, fi], [-fi, fr]])
    d, kind, f = np.meshgrid(np.arange(ndev), np.arange(2), np.arange(nf), indexing="ij")
    perm = np.zeros((ndev, 2 * nf, 2 * filters))
    perm[d, kind * nf + f, kind * filters + d * nf + f] = 1.0
    if 2 * nf % 8:
        wide = np.zeros((nb, ndev, nb, 2 * nf, 2 * filters))
        for j in range(nb):
            wide[j, :, j] = perm
        perm = wide.reshape(nb, ndev * nb * 2 * nf, 2 * filters)
    else:
        perm = perm.reshape(1, ndev * 2 * nf, 2 * filters)
    perm_taps = np.zeros((nb, ndev, nb, dup, nf, filters))
    own = filters // ch_count // nf
    sel = np.zeros((nb, own, nb, dup, nf, LANES))
    for j in range(nb):
        for g in range(nf):
            for dev in range(ndev):
                perm_taps[j, dev, j, :, g, dev * nf + g] = 1.0
            for dev in range(own):
                sel[j, dev, j, 0, g, dev * nf + g] = 1.0
    bf = ml_dtypes.bfloat16
    return (
        perm.astype(bf),
        perm_taps.reshape(nb, ndev * nb * dup * nf, filters).astype(bf),
        sel.reshape(nb, own * nb * dup * nf, LANES).astype(bf),
        halves(first),
        halves(first_taps),
        halves(last),
        halves(last_filt),
        halves(second),
        halves(second.T),
        twist.astype(np.float32),
    )


def split(x):
    head = x.astype(jnp.bfloat16)
    return head, (x - head.astype(jnp.float32)).astype(jnp.bfloat16)


def mm(x, y):
    return jnp.dot(x, y, preferred_element_type=jnp.float32)


def mm_nt(x, y):
    return lax.dot_general(x, y, (((1,), (1,)), ((), ())), preferred_element_type=jnp.float32)


def left_table(table, x):
    hi, lo = split(x)
    return mm(table[0], hi) + mm(table[0], lo) + mm(table[1], hi)


def right_table(x, table):
    hi, lo = split(x)
    return mm(hi, table[0]) + mm(lo, table[0]) + mm(hi, table[1])


def kernel(
    seq_count, ch_count, nf,
    q_ref, k_ref, v_ref, h_ref, gain_ref, u_ref,
    perm, perm_taps, sel, first, first_taps, last, last_filt, second, second_t, twist,
    mix_ref, gq_ref, gk_ref, gv_ref, gf_ref,
    tx, rx, txh, rxh, txo, rxo, txf, rxf,
    send_a, recv_a, send_h, recv_h, send_o, recv_o, send_f, recv_f,
):
    ndev = seq_count * ch_count
    local_rows, filters = h_ref.shape
    nb = local_rows // LANES
    q = 2 * nf
    own = rxf.shape[0]
    rows = seq_count * nb * q
    s, c = lax.axis_index("seq"), lax.axis_index("ch")
    me = s * ch_count + c
    f32 = jnp.float32

    barrier = pltpu.get_barrier_semaphore()

    def greet(i, _):
        p = lax.rem(me + i, ndev)
        pl.semaphore_signal(
            barrier, inc=1, device_id=(p // ch_count, lax.rem(p, ch_count)), device_id_type=MESH
        )
        return 0

    lax.fori_loop(1, ndev, greet, 0)

    acc = None
    for j in range(nb):
        hi, lo = split(h_ref[pl.ds(j * LANES, LANES), :])
        part = mm_nt(perm_taps[j], hi) + mm_nt(perm_taps[j], lo)
        acc = part if acc is None else acc + part
    txh[...] = acc.reshape(txh.shape)
    acc = None
    for j in range(nb):
        r = pl.ds(j * LANES, LANES)
        m = k_ref[r, :].astype(f32) * v_ref[r, :].astype(f32)
        g = u_ref[r, :].astype(f32) * q_ref[r, :].astype(f32)
        hi, lo = split(jnp.concatenate([m, g], axis=1))
        if perm.shape[0] == 1:
            part = mm_nt(perm[0], hi) + mm_nt(perm[0], lo)
            tx[:, j * q : (j + 1) * q, :] = part.reshape(ndev, q, LANES)
        else:
            part = mm_nt(perm[j], hi) + mm_nt(perm[j], lo)
            acc = part if acc is None else acc + part
    if acc is not None:
        tx[...] = acc.reshape(tx.shape)

    def copy_a(p, src):
        return pltpu.make_async_remote_copy(
            src_ref=tx.at[p],
            dst_ref=rx.at[lax.rem(src, ch_count), src // ch_count],
            send_sem=send_a.at[p],
            recv_sem=recv_a.at[src],
            device_id=(p // ch_count, lax.rem(p, ch_count)),
            device_id_type=MESH,
        )

    def copy_h(p, src):
        return pltpu.make_async_remote_copy(
            src_ref=txh.at[p * ch_count + c],
            dst_ref=rxh.at[src],
            send_sem=send_h.at[p],
            recv_sem=recv_h.at[src],
            device_id=(p, c),
            device_id_type=MESH,
        )

    def copy_o(p, src):
        return pltpu.make_async_remote_copy(
            src_ref=txo.at[lax.rem(p, ch_count), p // ch_count],
            dst_ref=rxo.at[src],
            send_sem=send_o.at[p],
            recv_sem=recv_o.at[src],
            device_id=(p // ch_count, lax.rem(p, ch_count)),
            device_id_type=MESH,
        )

    def copy_f(p, slot, target_c):
        return pltpu.make_async_remote_copy(
            src_ref=txf.at[p],
            dst_ref=rxf.at[slot],
            send_sem=send_f.at[p],
            recv_sem=recv_f.at[slot],
            device_id=(p, target_c),
            device_id_type=MESH,
        )

    pl.semaphore_wait(barrier, ndev - 1)

    def go(count, at, make):
        def step(i, _):
            make(lax.rem(at + i, count)).start()
            return 0

        lax.fori_loop(1, count, step, 0)

    def arrive(count, at, make):
        def step(i, _):
            make(lax.rem(at + count - i, count)).wait_recv()
            return 0

        lax.fori_loop(1, count, step, 0)

    def sent(count, at, make):
        def step(i, _):
            make(lax.rem(at + i, count)).wait_send()
            return 0

        lax.fori_loop(1, count, step, 0)

    go(seq_count, s, lambda p: copy_h(p, s))
    go(ndev, me, lambda p: copy_a(p, me))
    rx[c, s] = tx[me]
    rxh[s] = txh[me]

    tr, ti = twist[0], twist[1]

    def forward(a, lane):
        ar, ai = a[:rows, lane : lane + LANES], a[rows:, lane : lane + LANES]
        b = jnp.concatenate([ar * tr - ai * ti, ar * ti + ai * tr], axis=1)
        return right_table(b, second)

    def backward(y):
        y = right_table(y, second_t)
        yr, yi = y[:, :LANES], y[:, LANES:]
        return jnp.concatenate([yr * tr + yi * ti, yi * tr - yr * ti], axis=0)

    arrive(seq_count, s, lambda p: copy_h(p, p))
    spec = forward(left_table(first_taps, rxh[...].reshape(-1, LANES)), 0)
    kind = lax.rem(lax.broadcasted_iota(jnp.int32, (rows, LANES), 0), q) < nf
    hr = spec[:, :LANES]
    hi_ = jnp.where(kind, spec[:, LANES:], -spec[:, LANES:])

    arrive(ndev, me, lambda p: copy_a(p, p))
    filt_r = jnp.zeros((rows, LANES), f32)
    filt_i = jnp.zeros((rows, LANES), f32)
    for pair in range(0, ch_count, 2):
        x = jnp.concatenate(
            [rx[pair].reshape(rows, LANES), rx[pair + 1].reshape(rows, LANES)], axis=1
        )
        a = left_table(first, x)
        outs = []
        for half in range(2):
            z = forward(a, half * LANES)
            zr, zi = z[:, :LANES], z[:, LANES:]
            gr = pltpu.roll(zr, rows - nf, 0)
            gi = pltpu.roll(zi, rows - nf, 0)
            filt_r = filt_r + zr * gr + zi * gi
            filt_i = filt_i + zr * gi - zi * gr
            y = jnp.concatenate([hr * zr - hi_ * zi, hr * zi + hi_ * zr], axis=1)
            outs.append(backward(y))
        out = left_table(last, jnp.concatenate(outs, axis=1))
        txo[pair] = out[:, :LANES].reshape(txo.shape[1:])
        txo[pair + 1] = out[:, LANES:].reshape(txo.shape[1:])

    go(ndev, me, lambda p: copy_o(p, me))
    rxo[me] = txo[c, s]

    out = left_table(last_filt, backward(jnp.concatenate([filt_r, filt_i], axis=1)))
    txf[...] = out.reshape(txf.shape)
    slot, target_c = lax.rem(me, own), me // own

    go(seq_count, s, lambda p: copy_f(p, slot, target_c))

    @pl.when(target_c != c)
    def _():
        copy_f(s, slot, target_c).start()

    @pl.when(target_c == c)
    def _():
        rxf[slot] = txf[s]

    arrive(ndev, me, lambda p: copy_o(p, p))

    for j in range(nb):
        r = pl.ds(j * LANES, LANES)
        if perm.shape[0] == 1:
            got = rxo[:, j * q : (j + 1) * q, :].reshape(ndev * q, LANES)
        else:
            got = rxo[...].reshape(-1, LANES)
        hi, lo = split(got.T)
        table = perm[min(j, perm.shape[0] - 1)]
        got = mm(hi, table) + mm(lo, table)
        query, key = q_ref[r, :].astype(f32), k_ref[r, :].astype(f32)
        value, up = v_ref[r, :].astype(f32), u_ref[r, :].astype(f32)
        gain = gain_ref[...]
        pre = got[:, :filters] + gain * (key * value)
        back = got[:, filters:] + gain * (up * query)
        mix_ref[r, :] = (query * pre).astype(jnp.bfloat16)
        gq_ref[r, :] = (up * pre).astype(jnp.bfloat16)
        gk_ref[r, :] = (back * value).astype(jnp.bfloat16)
        gv_ref[r, :] = (back * key).astype(jnp.bfloat16)

    def filt_in(i, _):
        @pl.when(c * own + i != me)
        def _():
            copy_f(s, i, c).wait_recv()

        return 0

    lax.fori_loop(0, own, filt_in, 0)
    hi, lo = split(rxf[...].reshape(-1, LANES).T)
    for j in range(nb):
        got = mm(hi, sel[j]) + mm(lo, sel[j])
        gf_ref[pl.ds(j * LANES, LANES), :] = got[:, : gf_ref.shape[1]]

    sent(seq_count, s, lambda p: copy_h(p, s))
    sent(ndev, me, lambda p: copy_a(p, me))
    sent(ndev, me, lambda p: copy_o(p, me))
    sent(seq_count, s, lambda p: copy_f(p, slot, target_c))

    @pl.when(target_c != c)
    def _():
        copy_f(s, slot, target_c).wait_send()


def local(query_proj, key_proj, value_proj, filter_taps, skip_gain, grad_mixer):
    seq_count, ch_count = lax.axis_size("seq"), lax.axis_size("ch")
    ndev = seq_count * ch_count
    local_rows, filters = filter_taps.shape
    nb = local_rows // LANES
    nf = filters // ndev
    dup = max(1, 8 // (nb * nf))
    own = filters // ch_count // nf
    tabs = tables(seq_count, ch_count, nb, filters)
    ab, hb = nb * 2 * nf, nb * dup * nf
    f32, bf16 = jnp.float32, jnp.bfloat16
    vmem = pl.BlockSpec(memory_space=pltpu.VMEM)
    dma = pltpu.SemaphoreType.DMA
    wide = jax.ShapeDtypeStruct((local_rows, filters), bf16)
    return pl.pallas_call(
        functools.partial(kernel, seq_count, ch_count, nf),
        out_shape=(
            wide, wide, wide, wide,
            jax.ShapeDtypeStruct((local_rows, filters // ch_count), f32),
        ),
        in_specs=[vmem] * (6 + len(tabs)),
        out_specs=(vmem,) * 5,
        scratch_shapes=[
            pltpu.VMEM((ndev, ab, LANES), f32),
            pltpu.VMEM((ch_count, seq_count, ab, LANES), f32),
            pltpu.VMEM((ndev, hb, LANES), f32),
            pltpu.VMEM((seq_count, hb, LANES), f32),
            pltpu.VMEM((ch_count, seq_count, ab, LANES), f32),
            pltpu.VMEM((ndev, ab, LANES), f32),
            pltpu.VMEM((seq_count, hb, LANES), f32),
            pltpu.VMEM((own, hb, LANES), f32),
            dma((ndev,)), dma((ndev,)), dma((seq_count,)), dma((seq_count,)),
            dma((ndev,)), dma((ndev,)), dma((seq_count,)), dma((own,)),
        ],
        compiler_params=pltpu.CompilerParams(
            collective_id=0, has_side_effects=True, vmem_limit_bytes=48 * 2**20
        ),
    )(
        query_proj, key_proj, value_proj, filter_taps,
        skip_gain.reshape(1, filters), grad_mixer, *tabs,
    )


def solution(mesh):
    in_specs = (
        P("seq", "ch"),
        P("seq", "ch"),
        P("seq", "ch"),
        P("seq", None),
        P("ch"),
        P("seq", "ch"),
    )
    out_specs = (P("seq", "ch"), P("seq", "ch"), P("seq", "ch"), P("seq", "ch"), P("seq", "ch"))
    return jax.shard_map(local, mesh=mesh, in_specs=in_specs, out_specs=out_specs, check_vma=False)
```

time: 683 us -> 59.3 us (0.09); the launches traced: 672 us -> 58.8 us
  waiting for transfers between devices: 552 us -> 0 us
  matrix products: 54.1 us -> 0 us
  Pallas kernels: 0 us -> 39.8 us
  other arithmetic: 28.5 us -> 0 us
  between operations: 15.5 us -> 0.67 us
  starting transfers between devices: 10.9 us -> 0 us
  local copies, waits for them, and re-layouts: 10.8 us -> 18.2 us
    ppermute x12 -> x0, waiting for transfers between devices: 533 us -> none  [from_partner(): lax.ppermute(array, axis, [(i, i ^ 1 << distance) for i in range(lax.axis...]
    dot_general x8 -> x0, matrix products: 54.1 us -> none  [the longest x2 13.6 us: apply_table(): jnp.einsum(form, table_real, data_real, precision=HIGHEST)]
    pallas_call x0 -> x1, Pallas kernels: none -> 39.8 us  [local(): pl.pallas_call(functools.partial(kernel, seq_count, ch_count, nf), out_sh...]
    select_n x6 -> x0, other arithmetic: 21.4 us -> none  [the longest x3 10.8 us: cross_forward(): real_part = jnp.where(is_upper, diff_real, real_part + partner_real)]
    reduce_scatter x1 -> x0, waiting for transfers between devices: 18.9 us -> none  [local(): lax.psum_scatter(filt_field, 'ch', scatter_dimension=1, tiled=True) * scale]
    ppermute x12 -> x0, starting transfers between devices: 10.8 us -> none  [from_partner(): lax.ppermute(array, axis, [(i, i ^ 1 << distance) for i in range(lax.axis...]
    unnamed x25 -> x36, local copies, waits for them, and re-layouts: 9.37 us -> 17.5 us
  transfers between devices with their start and end apart: 13 -> 0, of which waited for: 13 -> 0; matrix products, arithmetic and copies ran while one was open for 1% -> 0% of each run, Pallas kernels for 0% -> 0%
where the time goes in v1:
time: 59.3 us; the launch traced here: 58.8 us
  Pallas kernels  39.8 us (67%)
  local copies, waits for them, and re-layouts  18.2 us (31%)
  between operations  0.67 us (1%)
    pallas_call x1, Pallas kernels, local(): pl.pallas_call(functools.partial(kernel, seq_count, ch_count, nf), out_sh...  39.8 us
    unnamed x36, local copies, waits for them, and re-layouts  17.5 us

profile of v1, /device:TPU:25, one launch (start us, length us, event | category | flops | bytes accessed | tf_op | source)
XLA Modules:
  0.0 58.8 jit_solution(6339397717264464830)
XLA Ops:
  0.6 0.0 copy-start.15
  0.6 0.6 %copy-done.15 = f32[128]{0:T(128)S(1)} copy-done((f32[128]{0:T(128)S(1)}, f32[128]{0:T(128)}, u32[]{:S(2)}) %copy-start.15) | copy-done | bytes 536
  1.3 0.0 copy-start
  1.3 1.0 %copy-done = bf16[2,256,512]{2,1,0:T(8,128)(2,1)S(1)} copy-done((bf16[2,256,512]{2,1,0:T(8,128)(2,1)S(1)}, bf16[2,256,512]{2,1,0:T(8,128)(2,1)}, u32[]{:S(2)}) %copy-start) | copy-done | bytes 524312
  2.3 0.0 copy-start.1
  2.3 1.0 %copy-done.1 = bf16[2,512,256]{2,1,0:T(8,128)(2,1)S(1)} copy-done((bf16[2,512,256]{2,1,0:T(8,128)(2,1)S(1)}, bf16[2,512,256]{2,1,0:T(8,128)(2,1)}, u32[]{:S(2)}) %copy-start.1) | copy-done | bytes 524312
  3.4 0.0 copy-start.2
  3.4 1.0 %copy-done.2 = bf16[4,512,128]{2,1,0:T(8,128)(2,1)S(1)} copy-done((bf16[4,512,128]{2,1,0:T(8,128)(2,1)S(1)}, bf16[4,512,128]{2,1,0:T(8,128)(2,1)}, u32[]{:S(2)}) %copy-start.2) | copy-done | bytes 524312
  4.4 0.0 copy-start.3
  4.4 0.9 %copy-done.3 = f32[512,128]{1,0:T(8,128)S(1)} copy-done((f32[512,128]{1,0:T(8,128)S(1)}, f32[512,128]{1,0:T(8,128)}, u32[]{:S(2)}) %copy-start.3) | copy-done | bytes 262168
  5.4 0.0 copy-start.4
  5.4 0.9 %copy-done.4 = f32[2,256,128]{2,1,0:T(8,128)S(1)} copy-done((f32[2,256,128]{2,1,0:T(8,128)S(1)}, f32[2,256,128]{2,1,0:T(8,128)}, u32[]{:S(2)}) %copy-start.4) | copy-done | bytes 262168
  6.3 0.0 copy-start.5
  6.3 0.9 %copy-done.5 = bf16[2,256,256]{2,1,0:T(8,128)(2,1)S(1)} copy-done((bf16[2,256,256]{2,1,0:T(8,128)(2,1)S(1)}, bf16[2,256,256]{2,1,0:T(8,128)(2,1)}, u32[]{:S(2)}) %copy-start.5) | copy-done | bytes 262168
  7.3 0.0 copy-start.6
  7.3 0.9 %copy-done.6 = bf16[2,256,256]{2,1,0:T(8,128)(2,1)S(1)} copy-done((bf16[2,256,256]{2,1,0:T(8,128)(2,1)S(1)}, bf16[2,256,256]{2,1,0:T(8,128)(2,1)}, u32[]{:S(2)}) %copy-start.6) | copy-done | bytes 262168
  8.2 0.0 copy-start.7
  8.2 0.9 %copy-done.7 = bf16[2,128,512]{2,1,0:T(8,128)(2,1)S(1)} copy-done((bf16[2,128,512]{2,1,0:T(8,128)(2,1)S(1)}, bf16[2,128,512]{2,1,0:T(8,128)(2,1)}, u32[]{:S(2)}) %copy-start.7) | copy-done | bytes 262168
  9.2 0.0 copy-start.8
  9.2 0.9 %copy-done.8 = bf16[2,512,128]{2,1,0:T(8,128)(2,1)S(1)} copy-done((bf16[2,512,128]{2,1,0:T(8,128)(2,1)S(1)}, bf16[2,512,128]{2,1,0:T(8,128)(2,1)}, u32[]{:S(2)}) %copy-start.8) | copy-done | bytes 262168
  10.1 0.0 copy-start.9
  10.1 0.9 %copy-done.9 = bf16[512,128]{1,0:T(8,128)(2,1)S(1)} copy-done((bf16[512,128]{1,0:T(8,128)(2,1)S(1)}, bf16[512,128]{1,0:T(8,128)(2,1)}, u32[]{:S(2)}) %copy-start.9) | copy-done | bytes 131096
  11.0 0.0 copy-start.10
  11.0 0.9 %copy-done.10 = bf16[512,128]{1,0:T(8,128)(2,1)S(1)} copy-done((bf16[512,128]{1,0:T(8,128)(2,1)S(1)}, bf16[512,128]{1,0:T(8,128)(2,1)}, u32[]{:S(2)}) %copy-start.10) | copy-done | bytes 131096
  11.9 0.0 copy-start.11
  11.9 0.9 %copy-done.11 = bf16[512,128]{1,0:T(8,128)(2,1)S(1)} copy-done((bf16[512,128]{1,0:T(8,128)(2,1)S(1)}, bf16[512,128]{1,0:T(8,128)(2,1)}, u32[]{:S(2)}) %copy-start.11) | copy-done | bytes 131096
  12.8 0.0 copy-start.12
  12.8 0.9 %copy-done.12 = bf16[512,128]{1,0:T(8,128)(2,1)S(1)} copy-done((bf16[512,128]{1,0:T(8,128)(2,1)S(1)}, bf16[512,128]{1,0:T(8,128)(2,1)}, u32[]{:S(2)}) %copy-start.12) | copy-done | bytes 131096
  13.7 0.0 copy-start.13
  13.7 0.9 %copy-done.13 = bf16[4,128,128]{2,1,0:T(8,128)(2,1)S(1)} copy-done((bf16[4,128,128]{2,1,0:T(8,128)(2,1)S(1)}, bf16[4,128,128]{2,1,0:T(8,128)(2,1)}, u32[]{:S(2)}) %copy-start.13) | copy-done | bytes 131096
  14.6 0.0 copy-start.14
  14.6 0.9 %copy-done.14 = bf16[1,256,256]{2,1,0:T(8,128)(2,1)S(1)} copy-done((bf16[1,256,256]{2,1,0:T(8,128)(2,1)S(1)}, bf16[1,256,256]{2,1,0:T(8,128)(2,1)}, u32[]{:S(2)}) %copy-start.14) | copy-done | bytes 131096
  15.5 39.8 %shard_map.191 = (bf16[512,128]{1,0:T(8,128)(2,1)S(1)}, bf16[512,128]{1,0:T(8,128)(2,1)S(1)}, bf16[512,128]{1,0:T(8,128)(2,1)S(1)}, bf16[512,128]{1,0:T(8,128)(2,1)S(1)}, f32[512,32]{1,0:T(8,128)S(1)}) custom-call(bf16[512,128]{1,0:T(8,128)(2,1)S(1)} %copy-done.9, bf16[512,128]{1,0:T(8,128)(2,1)S(1)} %copy-done.10, bf16[512,128]{1,0:T(8,128)(2,1)S(1)} %copy-done.11, ...), custom_call_target="tpu_custom_call" | custom-call | tf_op jit(solution)/shard_map/pallas_call | solution.py:335
  55.4 0.7 %copy.21 = f32[512,32]{0,1:T(8,128)} copy(f32[512,32]{1,0:T(8,128)S(1)} %get-tuple-element.9) | data formatting | bytes 131072 | tf_op jit(solution)/shard_map/pallas_call | solution.py:335
  56.1 0.7 %copy.26 = bf16[512,128]{1,0:T(8,128)(2,1)} copy(bf16[512,128]{1,0:T(8,128)(2,1)S(1)} %get-tuple-element.15) | data formatting | bytes 262144
  56.8 0.7 %copy.27 = bf16[512,128]{1,0:T(8,128)(2,1)} copy(bf16[512,128]{1,0:T(8,128)(2,1)S(1)} %get-tuple-element.16) | data formatting | bytes 262144
  57.4 0.7 %copy.28 = bf16[512,128]{1,0:T(8,128)(2,1)} copy(bf16[512,128]{1,0:T(8,128)(2,1)S(1)} %get-tuple-element.17) | data formatting | bytes 262144
  58.1 0.7 %copy.29 = bf16[512,128]{1,0:T(8,128)(2,1)} copy(bf16[512,128]{1,0:T(8,128)(2,1)S(1)} %get-tuple-element.18) | data formatting | bytes 262144
Async XLA Ops:
  0.6 0.7 %copy-start.15 = (f32[128]{0:T(128)S(1)}, f32[128]{0:T(128)}, u32[]{:S(2)}) copy-start(f32[128]{0:T(128)} %param.20) | copy-start | bytes 1540
  1.3 1.0 %copy-start = (bf16[2,256,512]{2,1,0:T(8,128)(2,1)S(1)}, bf16[2,256,512]{2,1,0:T(8,128)(2,1)}, u32[]{:S(2)}) copy-start(bf16[2,256,512]{2,1,0:T(8,128)(2,1)} %constant.25.clone.last) | copy-start | bytes 1572868
  2.3 1.0 %copy-start.1 = (bf16[2,512,256]{2,1,0:T(8,128)(2,1)S(1)}, bf16[2,512,256]{2,1,0:T(8,128)(2,1)}, u32[]{:S(2)}) copy-start(bf16[2,512,256]{2,1,0:T(8,128)(2,1)} %constant.23.clone.first) | copy-start | bytes 1572868
  3.4 1.0 %copy-start.2 = (bf16[4,512,128]{2,1,0:T(8,128)(2,1)S(1)}, bf16[4,512,128]{2,1,0:T(8,128)(2,1)}, u32[]{:S(2)}) copy-start(bf16[4,512,128]{2,1,0:T(8,128)(2,1)} %constant.21.clone.perm_taps) | copy-start | bytes 1572868
  4.4 0.9 %copy-start.3 = (f32[512,128]{1,0:T(8,128)S(1)}, f32[512,128]{1,0:T(8,128)}, u32[]{:S(2)}) copy-start(f32[512,128]{1,0:T(8,128)} %h_ref.1) | copy-start | bytes 786436
  5.4 0.9 %copy-start.4 = (f32[2,256,128]{2,1,0:T(8,128)S(1)}, f32[2,256,128]{2,1,0:T(8,128)}, u32[]{:S(2)}) copy-start(f32[2,256,128]{2,1,0:T(8,128)} %constant.29.clone.twist) | copy-start | bytes 786436
  6.3 0.9 %copy-start.5 = (bf16[2,256,256]{2,1,0:T(8,128)(2,1)S(1)}, bf16[2,256,256]{2,1,0:T(8,128)(2,1)}, u32[]{:S(2)}) copy-start(bf16[2,256,256]{2,1,0:T(8,128)(2,1)} %constant.28.clone.second_t) | copy-start | bytes 786436
  7.3 0.9 %copy-start.6 = (bf16[2,256,256]{2,1,0:T(8,128)(2,1)S(1)}, bf16[2,256,256]{2,1,0:T(8,128)(2,1)}, u32[]{:S(2)}) copy-start(bf16[2,256,256]{2,1,0:T(8,128)(2,1)} %constant.27.clone.second) | copy-start | bytes 786436
  8.2 0.9 %copy-start.7 = (bf16[2,128,512]{2,1,0:T(8,128)(2,1)S(1)}, bf16[2,128,512]{2,1,0:T(8,128)(2,1)}, u32[]{:S(2)}) copy-start(bf16[2,128,512]{2,1,0:T(8,128)(2,1)} %constant.26.clone.last_filt) | copy-start | bytes 786436
  9.2 0.9 %copy-start.8 = (bf16[2,512,128]{2,1,0:T(8,128)(2,1)S(1)}, bf16[2,512,128]{2,1,0:T(8,128)(2,1)}, u32[]{:S(2)}) copy-start(bf16[2,512,128]{2,1,0:T(8,128)(2,1)} %constant.24.clone.first_taps) | copy-start | bytes 786436
  10.1 0.9 %copy-start.9 = (bf16[512,128]{1,0:T(8,128)(2,1)S(1)}, bf16[512,128]{1,0:T(8,128)(2,1)}, u32[]{:S(2)}) copy-start(bf16[512,128]{1,0:T(8,128)(2,1)} %q_ref.1) | copy-start | bytes 393220
  11.0 0.9 %copy-start.10 = (bf16[512,128]{1,0:T(8,128)(2,1)S(1)}, bf16[512,128]{1,0:T(8,128)(2,1)}, u32[]{:S(2)}) copy-start(bf16[512,128]{1,0:T(8,128)(2,1)} %k_ref.1) | copy-start | bytes 393220
  11.9 0.9 %copy-start.11 = (bf16[512,128]{1,0:T(8,128)(2,1)S(1)}, bf16[512,128]{1,0:T(8,128)(2,1)}, u32[]{:S(2)}) copy-start(bf16[512,128]{1,0:T(8,128)(2,1)} %v_ref.1) | copy-start | bytes 393220
  12.8 0.9 %copy-start.12 = (bf16[512,128]{1,0:T(8,128)(2,1)S(1)}, bf16[512,128]{1,0:T(8,128)(2,1)}, u32[]{:S(2)}) copy-start(bf16[512,128]{1,0:T(8,128)(2,1)} %u_ref.1) | copy-start | bytes 393220
  13.7 0.9 %copy-start.13 = (bf16[4,128,128]{2,1,0:T(8,128)(2,1)S(1)}, bf16[4,128,128]{2,1,0:T(8,128)(2,1)}, u32[]{:S(2)}) copy-start(bf16[4,128,128]{2,1,0:T(8,128)(2,1)} %constant.22.clone.sel) | copy-start | bytes 393220
  14.6 0.9 %copy-start.14 = (bf16[1,256,256]{2,1,0:T(8,128)(2,1)S(1)}, bf16[1,256,256]{2,1,0:T(8,128)(2,1)}, u32[]{:S(2)}) copy-start(bf16[1,256,256]{2,1,0:T(8,128)(2,1)} %constant.20.clone.perm) | copy-start | bytes 393220

commit v2 on v1

--- a/solution.py
+++ b/solution.py
@@ -62,10 +62,10 @@
             for dev in range(own):
                 sel[j, dev, j, 0, g, dev * nf + g] = 1.0
     bf = ml_dtypes.bfloat16
+    perm_taps = perm_taps.reshape(nb, ndev * nb * dup * nf, filters).astype(bf)
     return (
         perm.astype(bf),
-        perm_taps.reshape(nb, ndev * nb * dup * nf, filters).astype(bf),
-        sel.reshape(nb, own * nb * dup * nf, LANES).astype(bf),
+        perm_taps[:, :16, :] if len(perm) == 1 else perm_taps,
         halves(first),
         halves(first_taps),
         halves(last),
@@ -73,6 +73,7 @@
         halves(second),
         halves(second.T),
         twist.astype(np.float32),
+        sel.reshape(nb, own * nb * dup * nf, LANES).astype(bf),
     )
 
 
@@ -101,12 +102,23 @@
 
 def kernel(
     seq_count, ch_count, nf,
-    q_ref, k_ref, v_ref, h_ref, gain_ref, u_ref,
-    perm, perm_taps, sel, first, first_taps, last, last_filt, second, second_t, twist,
-    mix_ref, gq_ref, gk_ref, gv_ref, gf_ref,
-    tx, rx, txh, rxh, txo, rxo, txf, rxf,
-    send_a, recv_a, send_h, recv_h, send_o, recv_o, send_f, recv_f,
+    *refs,
 ):
+    count = (len(refs) - 22) // 2
+    stored, held = refs[:count], refs[count + 5 : 2 * count + 5]
+    mix_ref, gq_ref, gk_ref, gv_ref, gf_ref = refs[count : count + 5]
+    (
+        tx, rx, txh, rxh, txo, rxo, txf, rxf,
+        send_a, recv_a, send_h, recv_h, send_o, recv_o, send_f, recv_f, load_sem,
+    ) = refs[2 * count + 5 :]
+    q_ref, k_ref, v_ref, u_ref, h_ref, perm, perm_taps = held[:7]
+    first, first_taps, last, last_filt, second, second_t, twist, sel, gain_ref = held[7:]
+    loads = [
+        pltpu.make_async_copy(src, dst, load_sem.at[i])
+        for i, (src, dst) in enumerate(zip(stored, held))
+    ]
+    for load in loads:
+        load.start()
     ndev = seq_count * ch_count
     local_rows, filters = h_ref.shape
     nb = local_rows // LANES
@@ -128,12 +140,22 @@
 
     lax.fori_loop(1, ndev, greet, 0)
 
-    acc = None
-    for j in range(nb):
-        hi, lo = split(h_ref[pl.ds(j * LANES, LANES), :])
-        part = mm_nt(perm_taps[j], hi) + mm_nt(perm_taps[j], lo)
-        acc = part if acc is None else acc + part
-    txh[...] = acc.reshape(txh.shape)
+    for load in loads[:7]:
+        load.wait()
+
+    if perm.shape[0] == 1:
+        for j in range(0, nb, 2):
+            both = [h_ref[pl.ds((j + e) * LANES, LANES), :] for e in range(2)]
+            hi, lo = split(jnp.concatenate(both, axis=1))
+            part = mm_nt(perm[0], hi) + mm_nt(perm[0], lo)
+            txh[:, j * nf : (j + 2) * nf, :] = part.reshape(ndev, q, LANES)
+    else:
+        acc = None
+        for j in range(nb):
+            hi, lo = split(h_ref[pl.ds(j * LANES, LANES), :])
+            part = mm_nt(perm_taps[j], hi) + mm_nt(perm_taps[j], lo)
+            acc = part if acc is None else acc + part
+        txh[...] = acc.reshape(txh.shape)
     acc = None
     for j in range(nb):
         r = pl.ds(j * LANES, LANES)
@@ -191,9 +213,12 @@
 
     pl.semaphore_wait(barrier, ndev - 1)
 
+    def stride(count):
+        return next(i for i in range(count * 2 // 5, count) if math.gcd(i, count) == 1)
+
     def go(count, at, make):
         def step(i, _):
-            make(lax.rem(at + i, count)).start()
+            make(lax.rem(at + i * stride(count), count)).start()
             return 0
 
         lax.fori_loop(1, count, step, 0)
@@ -217,6 +242,8 @@
     rx[c, s] = tx[me]
     rxh[s] = txh[me]
 
+    for load in loads[7:]:
+        load.wait()
     tr, ti = twist[0], twist[1]
 
     def forward(a, lane):
@@ -332,15 +359,20 @@
     vmem = pl.BlockSpec(memory_space=pltpu.VMEM)
     dma = pltpu.SemaphoreType.DMA
     wide = jax.ShapeDtypeStruct((local_rows, filters), bf16)
+    operands = (
+        query_proj, key_proj, value_proj, grad_mixer, filter_taps, *tabs,
+        skip_gain.reshape(1, filters),
+    )
     return pl.pallas_call(
         functools.partial(kernel, seq_count, ch_count, nf),
         out_shape=(
             wide, wide, wide, wide,
             jax.ShapeDtypeStruct((local_rows, filters // ch_count), f32),
         ),
-        in_specs=[vmem] * (6 + len(tabs)),
+        in_specs=[pl.BlockSpec(memory_space=pltpu.HBM)] * len(operands),
         out_specs=(vmem,) * 5,
-        scratch_shapes=[
+        scratch_shapes=[pltpu.VMEM(x.shape, x.dtype) for x in operands]
+        + [
             pltpu.VMEM((ndev, ab, LANES), f32),
             pltpu.VMEM((ch_count, seq_count, ab, LANES), f32),
             pltpu.VMEM((ndev, hb, LANES), f32),
@@ -351,14 +383,12 @@
             pltpu.VMEM((own, hb, LANES), f32),
             dma((ndev,)), dma((ndev,)), dma((seq_count,)), dma((seq_count,)),
             dma((ndev,)), dma((ndev,)), dma((seq_count,)), dma((own,)),
+            dma((len(operands),)),
         ],
         compiler_params=pltpu.CompilerParams(
             collective_id=0, has_side_effects=True, vmem_limit_bytes=48 * 2**20
         ),
-    )(
-        query_proj, key_proj, value_proj, filter_taps,
-        skip_gain.reshape(1, filters), grad_mixer, *tabs,
-    )
+    )(*operands)
 
 
 def solution(mesh):

time: 59.3 us -> 62.6 us (1.056)
  the two profiles are of different devices: /device:TPU:25 before, /device:TPU:0 now
where the time goes in v2:
time: 62.6 us; the launch traced here: 62.1 us
  Pallas kernels  43.5 us (69%)
  local copies, waits for them, and re-layouts  17.9 us (29%)
  between operations  0.67 us (1%)
    pallas_call x1, Pallas kernels, local(): pl.pallas_call(functools.partial(kernel, seq_count, ch_count, nf), out_sh...  43.5 us
    unnamed x36, local copies, waits for them, and re-layouts  17.2 us

profile of v2, /device:TPU:0, one launch (start us, length us, event | category | flops | bytes accessed | tf_op | source)
XLA Modules:
  0.0 62.1 jit_solution(9774922824673763986)
XLA Ops:
  0.6 0.0 copy-start.15
  0.6 0.6 %copy-done.15 = f32[128]{0:T(128)S(1)} copy-done((f32[128]{0:T(128)S(1)}, f32[128]{0:T(128)}, u32[]{:S(2)}) %copy-start.15) | copy-done | bytes 536
  1.3 0.0 copy-start
  1.3 1.0 %copy-done = bf16[2,256,512]{2,1,0:T(8,128)(2,1)S(1)} copy-done((bf16[2,256,512]{2,1,0:T(8,128)(2,1)S(1)}, bf16[2,256,512]{2,1,0:T(8,128)(2,1)}, u32[]{:S(2)}) %copy-start) | copy-done | bytes 524312
  2.3 0.0 copy-start.1
  2.3 1.0 %copy-done.1 = bf16[2,512,256]{2,1,0:T(8,128)(2,1)S(1)} copy-done((bf16[2,512,256]{2,1,0:T(8,128)(2,1)S(1)}, bf16[2,512,256]{2,1,0:T(8,128)(2,1)}, u32[]{:S(2)}) %copy-start.1) | copy-done | bytes 524312
  3.4 0.0 copy-start.2
  3.4 0.9 %copy-done.2 = f32[512,128]{1,0:T(8,128)S(1)} copy-done((f32[512,128]{1,0:T(8,128)S(1)}, f32[512,128]{1,0:T(8,128)}, u32[]{:S(2)}) %copy-start.2) | copy-done | bytes 262168
  4.3 0.0 copy-start.3
  4.3 0.9 %copy-done.3 = f32[2,256,128]{2,1,0:T(8,128)S(1)} copy-done((f32[2,256,128]{2,1,0:T(8,128)S(1)}, f32[2,256,128]{2,1,0:T(8,128)}, u32[]{:S(2)}) %copy-start.3) | copy-done | bytes 262168
  5.3 0.0 copy-start.4
  5.3 0.9 %copy-done.4 = bf16[2,256,256]{2,1,0:T(8,128)(2,1)S(1)} copy-done((bf16[2,256,256]{2,1,0:T(8,128)(2,1)S(1)}, bf16[2,256,256]{2,1,0:T(8,128)(2,1)}, u32[]{:S(2)}) %copy-start.4) | copy-done | bytes 262168
  6.2 0.0 copy-start.5
  6.2 0.9 %copy-done.5 = bf16[2,256,256]{2,1,0:T(8,128)(2,1)S(1)} copy-done((bf16[2,256,256]{2,1,0:T(8,128)(2,1)S(1)}, bf16[2,256,256]{2,1,0:T(8,128)(2,1)}, u32[]{:S(2)}) %copy-start.5) | copy-done | bytes 262168
  7.2 0.0 copy-start.6
  7.2 0.9 %copy-done.6 = bf16[2,128,512]{2,1,0:T(8,128)(2,1)S(1)} copy-done((bf16[2,128,512]{2,1,0:T(8,128)(2,1)S(1)}, bf16[2,128,512]{2,1,0:T(8,128)(2,1)}, u32[]{:S(2)}) %copy-start.6) | copy-done | bytes 262168
  8.1 0.0 copy-start.7
  8.1 0.9 %copy-done.7 = bf16[2,512,128]{2,1,0:T(8,128)(2,1)S(1)} copy-done((bf16[2,512,128]{2,1,0:T(8,128)(2,1)S(1)}, bf16[2,512,128]{2,1,0:T(8,128)(2,1)}, u32[]{:S(2)}) %copy-start.7) | copy-done | bytes 262168
  9.1 0.0 copy-start.8
  9.1 0.9 %copy-done.8 = bf16[512,128]{1,0:T(8,128)(2,1)S(1)} copy-done((bf16[512,128]{1,0:T(8,128)(2,1)S(1)}, bf16[512,128]{1,0:T(8,128)(2,1)}, u32[]{:S(2)}) %copy-start.8) | copy-done | bytes 131096
  10.0 0.0 copy-start.9
  10.0 0.9 %copy-done.9 = bf16[512,128]{1,0:T(8,128)(2,1)S(1)} copy-done((bf16[512,128]{1,0:T(8,128)(2,1)S(1)}, bf16[512,128]{1,0:T(8,128)(2,1)}, u32[]{:S(2)}) %copy-start.9) | copy-done | bytes 131096
  10.9 0.0 copy-start.10
  10.9 0.9 %copy-done.10 = bf16[512,128]{1,0:T(8,128)(2,1)S(1)} copy-done((bf16[512,128]{1,0:T(8,128)(2,1)S(1)}, bf16[512,128]{1,0:T(8,128)(2,1)}, u32[]{:S(2)}) %copy-start.10) | copy-done | bytes 131096
  11.8 0.0 copy-start.11
  11.8 0.9 %copy-done.11 = bf16[512,128]{1,0:T(8,128)(2,1)S(1)} copy-done((bf16[512,128]{1,0:T(8,128)(2,1)S(1)}, bf16[512,128]{1,0:T(8,128)(2,1)}, u32[]{:S(2)}) %copy-start.11) | copy-done | bytes 131096
  12.7 0.0 copy-start.12
  12.7 0.9 %copy-done.12 = bf16[4,128,128]{2,1,0:T(8,128)(2,1)S(1)} copy-done((bf16[4,128,128]{2,1,0:T(8,128)(2,1)S(1)}, bf16[4,128,128]{2,1,0:T(8,128)(2,1)}, u32[]{:S(2)}) %copy-start.12) | copy-done | bytes 131096
  13.6 0.0 copy-start.13
  13.6 0.9 %copy-done.13 = bf16[1,256,256]{2,1,0:T(8,128)(2,1)S(1)} copy-done((bf16[1,256,256]{2,1,0:T(8,128)(2,1)S(1)}, bf16[1,256,256]{2,1,0:T(8,128)(2,1)}, u32[]{:S(2)}) %copy-start.13) | copy-done | bytes 131096
  14.5 0.0 copy-start.14
  14.5 0.7 %copy-done.14 = bf16[4,16,128]{2,1,0:T(8,128)(2,1)S(1)} copy-done((bf16[4,16,128]{2,1,0:T(8,128)(2,1)S(1)}, bf16[4,16,128]{2,1,0:T(8,128)(2,1)}, u32[]{:S(2)}) %copy-start.14) | copy-done | bytes 16408
  15.2 43.5 %shard_map.191 = (bf16[512,128]{1,0:T(8,128)(2,1)S(1)}, bf16[512,128]{1,0:T(8,128)(2,1)S(1)}, bf16[512,128]{1,0:T(8,128)(2,1)S(1)}, bf16[512,128]{1,0:T(8,128)(2,1)S(1)}, f32[512,32]{1,0:T(8,128)S(1)}) custom-call(bf16[512,128]{1,0:T(8,128)(2,1)S(1)} %copy-done.8, bf16[512,128]{1,0:T(8,128)(2,1)S(1)} %copy-done.9, bf16[512,128]{1,0:T(8,128)(2,1)S(1)} %copy-done.10, ...), custom_call_target="tpu_custom_call" | custom-call | tf_op jit(solution)/shard_map/pallas_call | solution.py:366
  58.7 0.7 %copy.21 = f32[512,32]{0,1:T(8,128)} copy(f32[512,32]{1,0:T(8,128)S(1)} %get-tuple-element.9) | data formatting | bytes 131072 | tf_op jit(solution)/shard_map/pallas_call | solution.py:366
  59.5 0.7 %copy.26 = bf16[512,128]{1,0:T(8,128)(2,1)} copy(bf16[512,128]{1,0:T(8,128)(2,1)S(1)} %get-tuple-element.15) | data formatting | bytes 262144
  60.1 0.7 %copy.27 = bf16[512,128]{1,0:T(8,128)(2,1)} copy(bf16[512,128]{1,0:T(8,128)(2,1)S(1)} %get-tuple-element.16) | data formatting | bytes 262144
  60.8 0.7 %copy.28 = bf16[512,128]{1,0:T(8,128)(2,1)} copy(bf16[512,128]{1,0:T(8,128)(2,1)S(1)} %get-tuple-element.17) | data formatting | bytes 262144
  61.4 0.7 %copy.29 = bf16[512,128]{1,0:T(8,128)(2,1)} copy(bf16[512,128]{1,0:T(8,128)(2,1)S(1)} %get-tuple-element.18) | data formatting | bytes 262144
Async XLA Ops:
  0.6 0.7 %copy-start.15 = (f32[128]{0:T(128)S(1)}, f32[128]{0:T(128)}, u32[]{:S(2)}) copy-start(f32[128]{0:T(128)} %param.20) | copy-start | bytes 1540
  1.3 1.0 %copy-start = (bf16[2,256,512]{2,1,0:T(8,128)(2,1)S(1)}, bf16[2,256,512]{2,1,0:T(8,128)(2,1)}, u32[]{:S(2)}) copy-start(bf16[2,256,512]{2,1,0:T(8,128)(2,1)} %constant.24.clone.refs_9_) | copy-start | bytes 1572868
  2.3 1.0 %copy-start.1 = (bf16[2,512,256]{2,1,0:T(8,128)(2,1)S(1)}, bf16[2,512,256]{2,1,0:T(8,128)(2,1)}, u32[]{:S(2)}) copy-start(bf16[2,512,256]{2,1,0:T(8,128)(2,1)} %constant.22.clone.refs_7_) | copy-start | bytes 1572868
  3.4 0.9 %copy-start.2 = (f32[512,128]{1,0:T(8,128)S(1)}, f32[512,128]{1,0:T(8,128)}, u32[]{:S(2)}) copy-start(f32[512,128]{1,0:T(8,128)} %refs_4_.1) | copy-start | bytes 786436
  4.3 0.9 %copy-start.3 = (f32[2,256,128]{2,1,0:T(8,128)S(1)}, f32[2,256,128]{2,1,0:T(8,128)}, u32[]{:S(2)}) copy-start(f32[2,256,128]{2,1,0:T(8,128)} %constant.28.clone.refs_13_) | copy-start | bytes 786436
  5.3 0.9 %copy-start.4 = (bf16[2,256,256]{2,1,0:T(8,128)(2,1)S(1)}, bf16[2,256,256]{2,1,0:T(8,128)(2,1)}, u32[]{:S(2)}) copy-start(bf16[2,256,256]{2,1,0:T(8,128)(2,1)} %constant.27.clone.refs_12_) | copy-start | bytes 786436
  6.2 0.9 %copy-start.5 = (bf16[2,256,256]{2,1,0:T(8,128)(2,1)S(1)}, bf16[2,256,256]{2,1,0:T(8,128)(2,1)}, u32[]{:S(2)}) copy-start(bf16[2,256,256]{2,1,0:T(8,128)(2,1)} %constant.26.clone.refs_11_) | copy-start | bytes 786436
  7.2 0.9 %copy-start.6 = (bf16[2,128,512]{2,1,0:T(8,128)(2,1)S(1)}, bf16[2,128,512]{2,1,0:T(8,128)(2,1)}, u32[]{:S(2)}) copy-start(bf16[2,128,512]{2,1,0:T(8,128)(2,1)} %constant.25.clone.refs_10_) | copy-start | bytes 786436
  8.1 0.9 %copy-start.7 = (bf16[2,512,128]{2,1,0:T(8,128)(2,1)S(1)}, bf16[2,512,128]{2,1,0:T(8,128)(2,1)}, u32[]{:S(2)}) copy-start(bf16[2,512,128]{2,1,0:T(8,128)(2,1)} %constant.23.clone.refs_8_) | copy-start | bytes 786436
  9.1 0.9 %copy-start.8 = (bf16[512,128]{1,0:T(8,128)(2,1)S(1)}, bf16[512,128]{1,0:T(8,128)(2,1)}, u32[]{:S(2)}) copy-start(bf16[512,128]{1,0:T(8,128)(2,1)} %refs_0_.1) | copy-start | bytes 393220
  10.0 0.9 %copy-start.9 = (bf16[512,128]{1,0:T(8,128)(2,1)S(1)}, bf16[512,128]{1,0:T(8,128)(2,1)}, u32[]{:S(2)}) copy-start(bf16[512,128]{1,0:T(8,128)(2,1)} %refs_1_.1) | copy-start | bytes 393220
  10.9 0.9 %copy-start.10 = (bf16[512,128]{1,0:T(8,128)(2,1)S(1)}, bf16[512,128]{1,0:T(8,128)(2,1)}, u32[]{:S(2)}) copy-start(bf16[512,128]{1,0:T(8,128)(2,1)} %refs_2_.1) | copy-start | bytes 393220
  11.8 0.9 %copy-start.11 = (bf16[512,128]{1,0:T(8,128)(2,1)S(1)}, bf16[512,128]{1,0:T(8,128)(2,1)}, u32[]{:S(2)}) copy-start(bf16[512,128]{1,0:T(8,128)(2,1)} %refs_3_.1) | copy-start | bytes 393220
  12.7 0.9 %copy-start.12 = (bf16[4,128,128]{2,1,0:T(8,128)(2,1)S(1)}, bf16[4,128,128]{2,1,0:T(8,128)(2,1)}, u32[]{:S(2)}) copy-start(bf16[4,128,128]{2,1,0:T(8,128)(2,1)} %constant.29.clone.refs_14_) | copy-start | bytes 393220
  13.6 0.9 %copy-start.13 = (bf16[1,256,256]{2,1,0:T(8,128)(2,1)S(1)}, bf16[1,256,256]{2,1,0:T(8,128)(2,1)}, u32[]{:S(2)}) copy-start(bf16[1,256,256]{2,1,0:T(8,128)(2,1)} %constant.20.clone.refs_5_) | copy-start | bytes 393220
  14.5 0.7 %copy-start.14 = (bf16[4,16,128]{2,1,0:T(8,128)(2,1)S(1)}, bf16[4,16,128]{2,1,0:T(8,128)(2,1)}, u32[]{:S(2)}) copy-start(bf16[4,16,128]{2,1,0:T(8,128)(2,1)} %constant.21.clone.refs_6_) | copy-start | bytes 49156

commit v3 on v2

--- a/solution.py
+++ b/solution.py
@@ -12,6 +12,7 @@
 
 MESH = pl.DeviceIdType.MESH
 LANES = 128
+VMEM_BYTES = 64 * 2**20
 
 
 def halves(table):
@@ -54,13 +55,13 @@
         perm = perm.reshape(1, ndev * 2 * nf, 2 * filters)
     perm_taps = np.zeros((nb, ndev, nb, dup, nf, filters))
     own = filters // ch_count // nf
-    sel = np.zeros((nb, own, nb, dup, nf, LANES))
+    sel = np.zeros((nb, own * nf, own, nb, dup, nf))
     for j in range(nb):
         for g in range(nf):
             for dev in range(ndev):
                 perm_taps[j, dev, j, :, g, dev * nf + g] = 1.0
             for dev in range(own):
-                sel[j, dev, j, 0, g, dev * nf + g] = 1.0
+                sel[j, dev * nf + g, dev, j, 0, g] = 1.0
     bf = ml_dtypes.bfloat16
     perm_taps = perm_taps.reshape(nb, ndev * nb * dup * nf, filters).astype(bf)
     return (
@@ -73,8 +74,7 @@
         halves(second),
         halves(second.T),
         twist.astype(np.float32),
-        sel.reshape(nb, own * nb * dup * nf, LANES).astype(bf),
-    )
+    ), sel.reshape(nb, own * nf, own * nb * dup * nf).astype(bf)
 
 
 def split(x):
@@ -104,15 +104,15 @@
     seq_count, ch_count, nf,
     *refs,
 ):
-    count = (len(refs) - 22) // 2
-    stored, held = refs[:count], refs[count + 5 : 2 * count + 5]
-    mix_ref, gq_ref, gk_ref, gv_ref, gf_ref = refs[count : count + 5]
+    count = (len(refs) - 18) // 2
+    stored, held = refs[:count], refs[count + 2 : 2 * count + 2]
+    rxo, rxf = refs[count : count + 2]
     (
-        tx, rx, txh, rxh, txo, rxo, txf, rxf,
-        send_a, recv_a, send_h, recv_h, send_o, recv_o, send_f, recv_f, load_sem,
-    ) = refs[2 * count + 5 :]
+        tx, rx, txh, rxh, txo, txf,
+        send_a, recv_a, send_h, recv_h, send_o, recv_o, send_f, recv_f, load_sem, own_sem,
+    ) = refs[2 * count + 2 :]
     q_ref, k_ref, v_ref, u_ref, h_ref, perm, perm_taps = held[:7]
-    first, first_taps, last, last_filt, second, second_t, twist, sel, gain_ref = held[7:]
+    first, first_taps, last, last_filt, second, second_t, twist = held[7:]
     loads = [
         pltpu.make_async_copy(src, dst, load_sem.at[i])
         for i, (src, dst) in enumerate(zip(stored, held))
@@ -213,12 +213,9 @@
 
     pl.semaphore_wait(barrier, ndev - 1)
 
-    def stride(count):
-        return next(i for i in range(count * 2 // 5, count) if math.gcd(i, count) == 1)
-
     def go(count, at, make):
         def step(i, _):
-            make(lax.rem(at + i * stride(count), count)).start()
+            make(lax.rem(at + i, count)).start()
             return 0
 
         lax.fori_loop(1, count, step, 0)
@@ -285,7 +282,8 @@
         txo[pair + 1] = out[:, LANES:].reshape(txo.shape[1:])
 
     go(ndev, me, lambda p: copy_o(p, me))
-    rxo[me] = txo[c, s]
+    own_o = pltpu.make_async_copy(txo.at[c, s], rxo.at[me], own_sem.at[0])
+    own_o.start()
 
     out = left_table(last_filt, backward(jnp.concatenate([filt_r, filt_i], axis=1)))
     txf[...] = out.reshape(txf.shape)
@@ -299,10 +297,61 @@
 
     @pl.when(target_c == c)
     def _():
-        rxf[slot] = txf[s]
+        pltpu.make_async_copy(txf.at[s], rxf.at[slot], own_sem.at[1]).start()
 
     arrive(ndev, me, lambda p: copy_o(p, p))
 
+    def filt_in(i, _):
+        @pl.when(c * own + i != me)
+        def _():
+            copy_f(s, i, c).wait_recv()
+
+        return 0
+
+    lax.fori_loop(0, own, filt_in, 0)
+    sent(seq_count, s, lambda p: copy_h(p, s))
+    sent(ndev, me, lambda p: copy_a(p, me))
+    sent(ndev, me, lambda p: copy_o(p, me))
+    sent(seq_count, s, lambda p: copy_f(p, slot, target_c))
+
+    @pl.when(target_c != c)
+    def _():
+        copy_f(s, slot, target_c).wait_send()
+
+    @pl.when(target_c == c)
+    def _():
+        pltpu.make_async_copy(txf.at[s], rxf.at[slot], own_sem.at[1]).wait()
+
+    own_o.wait()
+
+
+def finish(nf, *refs):
+    stored, drained = refs[:9], refs[9:14]
+    held, made = refs[14:23], refs[23:28]
+    load_sem, store_sem = refs[28:]
+    loads = [
+        pltpu.make_async_copy(src, dst, load_sem.at[i])
+        for i, (src, dst) in enumerate(zip(stored, held))
+    ]
+    for load in loads:
+        load.start()
+    stores = [
+        pltpu.make_async_copy(src, dst, store_sem.at[i])
+        for i, (src, dst) in enumerate(zip(made, drained))
+    ]
+    rxo, perm, q_ref, k_ref, v_ref, u_ref, gain_ref, rxf, sel = held
+    mix_ref, gq_ref, gk_ref, gv_ref, gf_ref = made
+    local_rows, filters = q_ref.shape
+    nb = local_rows // LANES
+    q = 2 * nf
+    ndev = rxo.shape[0]
+    f32 = jnp.float32
+    for load in loads:
+        load.wait()
+    hi, lo = split(rxf[...].reshape(-1, LANES))
+    for j in range(nb):
+        gf_ref[:, j * LANES : (j + 1) * LANES] = mm(sel[j], hi) + mm(sel[j], lo)
+    stores[4].start()
     for j in range(nb):
         r = pl.ds(j * LANES, LANES)
         if perm.shape[0] == 1:
@@ -321,28 +370,10 @@
         gq_ref[r, :] = (up * pre).astype(jnp.bfloat16)
         gk_ref[r, :] = (back * value).astype(jnp.bfloat16)
         gv_ref[r, :] = (back * key).astype(jnp.bfloat16)
-
-    def filt_in(i, _):
-        @pl.when(c * own + i != me)
-        def _():
-            copy_f(s, i, c).wait_recv()
-
-        return 0
-
-    lax.fori_loop(0, own, filt_in, 0)
-    hi, lo = split(rxf[...].reshape(-1, LANES).T)
-    for j in range(nb):
-        got = mm(hi, sel[j]) + mm(lo, sel[j])
-        gf_ref[pl.ds(j * LANES, LANES), :] = got[:, : gf_ref.shape[1]]
-
-    sent(seq_count, s, lambda p: copy_h(p, s))
-    sent(ndev, me, lambda p: copy_a(p, me))
-    sent(ndev, me, lambda p: copy_o(p, me))
-    sent(seq_count, s, lambda p: copy_f(p, slot, target_c))
-
-    @pl.when(target_c != c)
-    def _():
-        copy_f(s, slot, target_c).wait_send()
+    for store in stores[:4]:
+        store.start()
+    for store in stores:
+        store.wait()
 
 
 def local(query_proj, key_proj, value_proj, filter_taps, skip_gain, grad_mixer):
@@ -353,24 +384,20 @@
     nf = filters // ndev
     dup = max(1, 8 // (nb * nf))
     own = filters // ch_count // nf
-    tabs = tables(seq_count, ch_count, nb, filters)
+    tabs, sel = tables(seq_count, ch_count, nb, filters)
     ab, hb = nb * 2 * nf, nb * dup * nf
     f32, bf16 = jnp.float32, jnp.bfloat16
-    vmem = pl.BlockSpec(memory_space=pltpu.VMEM)
+    hbm = pl.BlockSpec(memory_space=pltpu.HBM)
     dma = pltpu.SemaphoreType.DMA
-    wide = jax.ShapeDtypeStruct((local_rows, filters), bf16)
-    operands = (
-        query_proj, key_proj, value_proj, grad_mixer, filter_taps, *tabs,
-        skip_gain.reshape(1, filters),
-    )
-    return pl.pallas_call(
+    operands = (query_proj, key_proj, value_proj, grad_mixer, filter_taps, *tabs)
+    home, filt = pl.pallas_call(
         functools.partial(kernel, seq_count, ch_count, nf),
         out_shape=(
-            wide, wide, wide, wide,
-            jax.ShapeDtypeStruct((local_rows, filters // ch_count), f32),
+            jax.ShapeDtypeStruct((ndev, ab, LANES), f32),
+            jax.ShapeDtypeStruct((own, hb, LANES), f32),
         ),
-        in_specs=[pl.BlockSpec(memory_space=pltpu.HBM)] * len(operands),
-        out_specs=(vmem,) * 5,
+        in_specs=[hbm] * len(operands),
+        out_specs=(hbm,) * 2,
         scratch_shapes=[pltpu.VMEM(x.shape, x.dtype) for x in operands]
         + [
             pltpu.VMEM((ndev, ab, LANES), f32),
@@ -378,17 +405,31 @@
             pltpu.VMEM((ndev, hb, LANES), f32),
             pltpu.VMEM((seq_count, hb, LANES), f32),
             pltpu.VMEM((ch_count, seq_count, ab, LANES), f32),
-            pltpu.VMEM((ndev, ab, LANES), f32),
             pltpu.VMEM((seq_count, hb, LANES), f32),
-            pltpu.VMEM((own, hb, LANES), f32),
             dma((ndev,)), dma((ndev,)), dma((seq_count,)), dma((seq_count,)),
             dma((ndev,)), dma((ndev,)), dma((seq_count,)), dma((own,)),
-            dma((len(operands),)),
+            dma((len(operands),)), dma((2,)),
         ],
         compiler_params=pltpu.CompilerParams(
-            collective_id=0, has_side_effects=True, vmem_limit_bytes=48 * 2**20
+            collective_id=0, has_side_effects=True, vmem_limit_bytes=VMEM_BYTES
         ),
     )(*operands)
+    wide = jax.ShapeDtypeStruct((local_rows, filters), bf16)
+    results = (wide, wide, wide, wide, jax.ShapeDtypeStruct((own * nf, local_rows), f32))
+    operands = (
+        home, tabs[0], query_proj, key_proj, value_proj, grad_mixer,
+        skip_gain.reshape(1, filters), filt, sel,
+    )
+    *outs, grad_filter = pl.pallas_call(
+        functools.partial(finish, nf),
+        out_shape=results,
+        in_specs=[hbm] * len(operands),
+        out_specs=(hbm,) * 5,
+        scratch_shapes=[pltpu.VMEM(x.shape, x.dtype) for x in operands + results]
+        + [dma((len(operands),)), dma((5,))],
+        compiler_params=pltpu.CompilerParams(vmem_limit_bytes=VMEM_BYTES),
+    )(*operands)
+    return (*outs, grad_filter.T)
 
 
 def solution(mesh):

time: 62.6 us -> 43.3 us (0.69)
  the two profiles are of different devices: /device:TPU:0 before, /device:TPU:25 now
where the time goes in v3:
time: 43.3 us; the launch traced here: 43.2 us
  Pallas kernels  42.5 us (98%)
  between operations  0.64 us (1%)
    pallas_call x1, Pallas kernels, local(): pl.pallas_call(functools.partial(kernel, seq_count, ch_count, nf), out_sh...  40 us
    pallas_call x1, Pallas kernels, local(): pl.pallas_call(functools.partial(finish, nf), out_shape=results, in_specs...  2.54 us

profile of v3, /device:TPU:25, one launch (start us, length us, event | category | flops | bytes accessed | tf_op | source)
XLA Modules:
  0.0 43.2 jit_solution(10589360962804229250)
XLA Ops:
  0.6 40.0 %shard_map.191 = (f32[32,32,128]{2,1,0:T(8,128)}, f32[8,16,128]{2,1,0:T(8,128)}) custom-call(bf16[512,128]{1,0:T(8,128)(2,1)} %refs_2_.3, bf16[512,128]{1,0:T(8,128)(2,1)} %refs_3_.3, bf16[512,128]{1,0:T(8,128)(2,1)} %refs_4_.3, bf16[512,128]{1,0:T(8,128)(2,1)} %refs_5_.2, f32[512,128]{1,0:T(8,128)} %refs_4_.2, ...), custom_call_target="tpu_custom_call" | custom-call | tf_op jit(solution)/shard_map/pallas_call | solution.py:393
  40.6 2.5 %shard_map.192 = (bf16[512,128]{1,0:T(8,128)(2,1)}, bf16[512,128]{1,0:T(8,128)(2,1)}, bf16[512,128]{1,0:T(8,128)(2,1)}, bf16[512,128]{1,0:T(8,128)(2,1)}, f32[32,512]{1,0:T(8,128)}) custom-call(f32[32,32,128]{2,1,0:T(8,128)} %get-tuple-element.12.refs_0_, bf16[1,256,256]{2,1,0:T(8,128)(2,1)} %constant.20.clone.refs_5_.refs_1_, bf16[512,128]{1,0:T(8,128)(2,1)} %refs_2_.3, ...), custom_call_target="tpu_custom_call" | custom-call | tf_op jit(solution)/shard_map/pallas_call | solution.py:423

commit v4 on v3

v4 whole, which is shorter than its diff:
```python
import functools
import math

import jax
import jax.numpy as jnp
import ml_dtypes
import numpy as np
from jax import lax
from jax.experimental import pallas as pl
from jax.experimental.pallas import tpu as pltpu
from jax.sharding import PartitionSpec as P

MESH = pl.DeviceIdType.MESH
LANES = 128
VMEM_BYTES = 64 * 2**20


def chunking(nf):
    chunks = 2 if nf % 4 == 0 else 1
    return chunks, nf // chunks


def halves(table):
    head = table.astype(np.float32).astype(ml_dtypes.bfloat16)
    tail = (table - head.astype(np.float64)).astype(np.float32).astype(ml_dtypes.bfloat16)
    return np.stack([head, tail])


@functools.lru_cache(maxsize=4)
def tables(seq_count, ch_count, nb, filters):
    ndev = seq_count * ch_count
    nf = filters // ndev
    dup = max(1, 8 // (nb * nf))
    n1 = seq_count * nb
    total = n1 * LANES
    a = np.arange(n1)
    ang = 2 * np.pi / n1 * ((a[:, None] + 0.25) * a[None, :])
    stack = np.concatenate([np.cos(ang), -np.sin(ang)], 0)
    chunks, part = chunking(nf)
    first = np.kron(stack, np.eye(2 * part))
    last = first.T / total
    stack = stack.reshape(2, n1, n1)
    owner = np.eye(nf).reshape(chunks, part, nf)
    one = np.eye(dup)[0]
    first_taps = np.einsum("rkn,bpf,q,d->rbkqpndf", stack, owner, np.ones(2), one)
    first_taps = first_taps.reshape(2 * chunks * n1 * 2 * part, n1 * dup * nf)
    last_filt = np.einsum("rkn,bpf,q,d->ndfrbkqp", stack, owner, np.eye(2)[0], np.ones(dup))
    last_filt = last_filt.reshape(n1 * dup * nf, -1) / total / math.sqrt(total)
    b = np.arange(LANES)
    turn = 2 * np.pi / total * ((a[:, None] + 0.25) * b[None, :])
    twist = np.repeat(np.stack([np.cos(turn), -np.sin(turn)]), 2 * part, axis=1)
    ang2 = 2 * np.pi / LANES * (b[:, None] * b[None, :] % LANES)
    fr, fi = np.cos(ang2), -np.sin(ang2)
    second = np.block([[fr, fi], [-fi, fr]])
    place = np.eye(filters).reshape(ndev, chunks, part, filters)
    group = max(1, 8 // (2 * part))
    perm = np.einsum("dbpc,ij,kl->bdikpjlc", place, np.eye(group), np.eye(2))
    perm = perm.reshape(chunks * ndev * group * 2 * part, group * 2 * filters)
    group = max(1, 8 // (nf * dup))
    place = np.eye(filters).reshape(ndev, nf, filters)
    perm_taps = np.einsum("dfc,ij,e->diefjc", place, np.eye(group), np.ones(dup))
    perm_taps = perm_taps.reshape(ndev * group * dup * nf, group * filters)
    own = filters // ch_count // nf
    sel = np.zeros((nb, own * nf, own, nb, dup, nf))
    for j in range(nb):
        for g in range(nf):
            for dev in range(own):
                sel[j, dev * nf + g, dev, j, 0, g] = 1.0
    bf = ml_dtypes.bfloat16
    return (
        perm.astype(bf),
        perm_taps.astype(bf),
        halves(first),
        halves(first_taps),
        halves(last),
        halves(last_filt),
        halves(second),
        halves(second.T),
        twist.astype(np.float32),
    ), sel.reshape(nb, own * nf, own * nb * dup * nf).astype(bf)


def split(x):
    head = x.astype(jnp.bfloat16)
    return head, (x - head.astype(jnp.float32)).astype(jnp.bfloat16)


def mm(x, y):
    return jnp.dot(x, y, preferred_element_type=jnp.float32)


def mm_nt(x, y):
    return lax.dot_general(x, y, (((1,), (1,)), ((), ())), preferred_element_type=jnp.float32)


def left_table(table, x):
    hi, lo = split(x)
    return mm(table[0], hi) + mm(table[0], lo) + mm(table[1], hi)


def right_table(x, table):
    hi, lo = split(x)
    return mm(hi, table[0]) + mm(lo, table[0]) + mm(hi, table[1])


def kernel(
    seq_count, ch_count, nf,
    *refs,
):
    count = (len(refs) - 18) // 2
    stored, held = refs[:count], refs[count + 2 : 2 * count + 2]
    rxo, rxf = refs[count : count + 2]
    (
        tx, rx, txh, rxh, txo, txf,
        send_a, recv_a, send_h, recv_h, send_o, recv_o, send_f, recv_f, load_sem, own_sem,
    ) = refs[2 * count + 2 :]
    q_ref, k_ref, v_ref, u_ref, h_ref, perm, perm_taps = held[:7]
    first, first_taps, last, last_filt, second, second_t, twist = held[7:]
    loads = [
        pltpu.make_async_copy(src, dst, load_sem.at[i])
        for i, (src, dst) in enumerate(zip(stored, held))
    ]
    for load in loads:
        load.start()
    ndev = seq_count * ch_count
    local_rows, filters = h_ref.shape
    nb = local_rows // LANES
    chunks, part = chunking(nf)
    q = 2 * part
    own = rxf.shape[0]
    rows = seq_count * nb * q
    s, c = lax.axis_index("seq"), lax.axis_index("ch")
    me = s * ch_count + c
    f32 = jnp.float32

    barrier = pltpu.get_barrier_semaphore()

    def greet(i, _):
        p = lax.rem(me + i, ndev)
        pl.semaphore_signal(
            barrier, inc=1, device_id=(p // ch_count, lax.rem(p, ch_count)), device_id_type=MESH
        )
        return 0

    lax.fori_loop(1, ndev, greet, 0)

    for load in loads[:7]:
        load.wait()

    def turn(table, blocks):
        hi, lo = split(jnp.concatenate(blocks, axis=1))
        return mm_nt(table[...], hi) + mm_nt(table[...], lo)

    width = perm_taps.shape[1] // filters
    for j in range(0, nb, width):
        out = turn(perm_taps, [h_ref[pl.ds((j + e) * LANES, LANES), :] for e in range(width)])
        at = j // width * 8
        txh[:, at : at + 8, :] = out.reshape(ndev, 8, LANES)

    def send_products():
        width = perm.shape[1] // (2 * filters)
        for j in range(0, nb, width):
            blocks = []
            for e in range(width):
                r = pl.ds((j + e) * LANES, LANES)
                blocks.append(k_ref[r, :].astype(f32) * v_ref[r, :].astype(f32))
                blocks.append(u_ref[r, :].astype(f32) * q_ref[r, :].astype(f32))
            at = j // width * 8
            tx[:, :, at : at + 8, :] = turn(perm, blocks).reshape(chunks, ndev, 8, LANES)

    send_products()

    def copy_a(b, p, src):
        return pltpu.make_async_remote_copy(
            src_ref=tx.at[b, p],
            dst_ref=rx.at[b, lax.rem(src, ch_count), src // ch_count],
            send_sem=send_a.at[b, p],
            recv_sem=recv_a.at[b, src],
            device_id=(p // ch_count, lax.rem(p, ch_count)),
            device_id_type=MESH,
        )

    def copy_h(p, src):
        return pltpu.make_async_remote_copy(
            src_ref=txh.at[p * ch_count + c],
            dst_ref=rxh.at[src],
            send_sem=send_h.at[p],
            recv_sem=recv_h.at[src],
            device_id=(p, c),
            device_id_type=MESH,
        )

    def copy_o(b, p, src):
        return pltpu.make_async_remote_copy(
            src_ref=txo.at[b, lax.rem(p, ch_count), p // ch_count],
            dst_ref=rxo.at[b, src],
            send_sem=send_o.at[b, p],
            recv_sem=recv_o.at[b, src],
            device_id=(p // ch_count, lax.rem(p, ch_count)),
            device_id_type=MESH,
        )

    def copy_f(p, slot, target_c):
        return pltpu.make_async_remote_copy(
            src_ref=txf.at[p],
            dst_ref=rxf.at[slot],
            send_sem=send_f.at[p],
            recv_sem=recv_f.at[slot],
            device_id=(p, target_c),
            device_id_type=MESH,
        )

    pl.semaphore_wait(barrier, ndev - 1)

    def go(count, at, make):
        def step(i, _):
            make(lax.rem(at + i, count)).start()
            return 0

        lax.fori_loop(1, count, step, 0)

    def arrive(count, at, make):
        def step(i, _):
            make(lax.rem(at + count - i, count)).wait_recv()
            return 0

        lax.fori_loop(1, count, step, 0)

    def sent(count, at, make):
        def step(i, _):
            make(lax.rem(at + i, count)).wait_send()
            return 0

        lax.fori_loop(1, count, step, 0)

    go(seq_count, s, lambda p: copy_h(p, s))
    for b in range(chunks):
        go(ndev, me, lambda p: copy_a(b, p, me))
        rx[b, c, s] = tx[b, me]
    rxh[s] = txh[me]

    for load in loads[7:]:
        load.wait()
    tr, ti = twist[0], twist[1]

    def forward(ar, ai, times):
        tr2, ti2 = jnp.concatenate([tr] * times, axis=0), jnp.concatenate([ti] * times, axis=0)
        b = jnp.concatenate([ar * tr2 - ai * ti2, ar * ti2 + ai * tr2], axis=1)
        z = right_table(b, second)
        return z[:, :LANES], z[:, LANES:]

    def backward(yr, yi, times):
        tr2, ti2 = jnp.concatenate([tr] * times, axis=0), jnp.concatenate([ti] * times, axis=0)
        y = right_table(jnp.concatenate([yr, yi], axis=1), second_t)
        yr, yi = y[:, :LANES], y[:, LANES:]
        return yr * tr2 + yi * ti2, yi * tr2 - yr * ti2

    arrive(seq_count, s, lambda p: copy_h(p, p))
    a = left_table(first_taps, rxh[...].reshape(-1, LANES))
    taps_r, taps_i = forward(a[: chunks * rows], a[chunks * rows :], chunks)
    kind = lax.rem(lax.broadcasted_iota(jnp.int32, (chunks * rows, LANES), 0), q) < part
    taps_i = jnp.where(kind, taps_i, -taps_i)

    filts_r, filts_i, own_o = [], [], []
    for b in range(chunks):
        arrive(ndev, me, lambda p: copy_a(b, p, p))
        hr, hi_ = taps_r[b * rows : (b + 1) * rows], taps_i[b * rows : (b + 1) * rows]
        hr, hi_ = jnp.concatenate([hr, hr], axis=0), jnp.concatenate([hi_, hi_], axis=0)
        filt_r = jnp.zeros((rows, LANES), f32)
        filt_i = jnp.zeros((rows, LANES), f32)
        for pair in range(0, ch_count, 2):
            x = jnp.concatenate(
                [rx[b, pair].reshape(rows, LANES), rx[b, pair + 1].reshape(rows, LANES)], axis=1
            )
            a = left_table(first, x)
            zr, zi = forward(
                jnp.concatenate([a[:rows, :LANES], a[:rows, LANES:]], axis=0),
                jnp.concatenate([a[rows:, :LANES], a[rows:, LANES:]], axis=0),
                2,
            )
            gr = pltpu.roll(zr, 2 * rows - part, 0)
            gi = pltpu.roll(zi, 2 * rows - part, 0)
            cr, ci = zr * gr + zi * gi, zr * gi - zi * gr
            filt_r = filt_r + cr[:rows] + cr[rows:]
            filt_i = filt_i + ci[:rows] + ci[rows:]
            dr, di = backward(hr * zr - hi_ * zi, hr * zi + hi_ * zr, 2)
            d = jnp.concatenate(
                [
                    jnp.concatenate([dr[:rows], dr[rows:]], axis=1),
                    jnp.concatenate([di[:rows], di[rows:]], axis=1),
                ],
                axis=0,
            )
            out = left_table(last, d)
            txo[b, pair] = out[:, :LANES].reshape(txo.shape[2:])
            txo[b, pair + 1] = out[:, LANES:].reshape(txo.shape[2:])
        filts_r.append(filt_r)
        filts_i.append(filt_i)
        go(ndev, me, lambda p: copy_o(b, p, me))
        keep = pltpu.make_async_copy(txo.at[b, c, s], rxo.at[b, me], own_sem.at[b + 1])
        keep.start()
        own_o.append(keep)

    dr, di = backward(
        jnp.concatenate(filts_r, axis=0), jnp.concatenate(filts_i, axis=0), chunks
    )
    out = left_table(last_filt, jnp.concatenate([dr, di], axis=0))
    txf[...] = out.reshape(txf.shape)
    slot, target_c = lax.rem(me, own), me // own

    go(seq_count, s, lambda p: copy_f(p, slot, target_c))

    @pl.when(target_c != c)
    def _():
        copy_f(s, slot, target_c).start()

    @pl.when(target_c == c)
    def _():
        pltpu.make_async_copy(txf.at[s], rxf.at[slot], own_sem.at[0]).start()

    for b in range(chunks):
        arrive(ndev, me, lambda p: copy_o(b, p, p))

    def filt_in(i, _):
        @pl.when(c * own + i != me)
        def _():
            copy_f(s, i, c).wait_recv()

        return 0

    lax.fori_loop(0, own, filt_in, 0)
    sent(seq_count, s, lambda p: copy_h(p, s))
    for b in range(chunks):
        sent(ndev, me, lambda p: copy_a(b, p, me))
        sent(ndev, me, lambda p: copy_o(b, p, me))
    sent(seq_count, s, lambda p: copy_f(p, slot, target_c))

    @pl.when(target_c != c)
    def _():
        copy_f(s, slot, target_c).wait_send()

    @pl.when(target_c == c)
    def _():
        pltpu.make_async_copy(txf.at[s], rxf.at[slot], own_sem.at[0]).wait()

    for keep in own_o:
        keep.wait()


def finish(*refs):
    stored, drained = refs[:9], refs[9:14]
    held, made = refs[14:23], refs[23:28]
    load_sem, store_sem = refs[28:]
    loads = [
        pltpu.make_async_copy(src, dst, load_sem.at[i])
        for i, (src, dst) in enumerate(zip(stored, held))
    ]
    for load in loads:
        load.start()
    stores = [
        pltpu.make_async_copy(src, dst, store_sem.at[i])
        for i, (src, dst) in enumerate(zip(made, drained))
    ]
    rxo, perm, q_ref, k_ref, v_ref, u_ref, gain_ref, rxf, sel = held
    mix_ref, gq_ref, gk_ref, gv_ref, gf_ref = made
    local_rows, filters = q_ref.shape
    nb = local_rows // LANES
    width = perm.shape[1] // (2 * filters)
    f32 = jnp.float32
    for load in loads:
        load.wait()
    hi, lo = split(rxf[...].reshape(-1, LANES))
    for j in range(nb):
        gf_ref[:, j * LANES : (j + 1) * LANES] = mm(sel[j], hi) + mm(sel[j], lo)
    stores[4].start()
    for j in range(nb):
        r = pl.ds(j * LANES, LANES)
        if j % width == 0:
            at = j // width * 8
            hi, lo = split(rxo[:, :, at : at + 8, :].reshape(-1, LANES).T)
            both = mm(hi, perm[...]) + mm(lo, perm[...])
        at = j % width * 2 * filters
        got = both[:, at : at + 2 * filters]
        query, key = q_ref[r, :].astype(f32), k_ref[r, :].astype(f32)
        value, up = v_ref[r, :].astype(f32), u_ref[r, :].astype(f32)
        gain = gain_ref[...]
        pre = got[:, :filters] + gain * (key * value)
        back = got[:, filters:] + gain * (up * query)
        mix_ref[r, :] = (query * pre).astype(jnp.bfloat16)
        gq_ref[r, :] = (up * pre).astype(jnp.bfloat16)
        gk_ref[r, :] = (back * value).astype(jnp.bfloat16)
        gv_ref[r, :] = (back * key).astype(jnp.bfloat16)
    for store in stores[:4]:
        store.start()
    for store in stores:
        store.wait()


def local(query_proj, key_proj, value_proj, filter_taps, skip_gain, grad_mixer):
    seq_count, ch_count = lax.axis_size("seq"), lax.axis_size("ch")
    ndev = seq_count * ch_count
    local_rows, filters = filter_taps.shape
    nb = local_rows // LANES
    nf = filters // ndev
    dup = max(1, 8 // (nb * nf))
    own = filters // ch_count // nf
    tabs, sel = tables(seq_count, ch_count, nb, filters)
    chunks, part = chunking(nf)
    ab, hb = nb * 2 * part, nb * dup * nf
    f32, bf16 = jnp.float32, jnp.bfloat16
    hbm = pl.BlockSpec(memory_space=pltpu.HBM)
    dma = pltpu.SemaphoreType.DMA
    operands = (query_proj, key_proj, value_proj, grad_mixer, filter_taps, *tabs)
    home, filt = pl.pallas_call(
        functools.partial(kernel, seq_count, ch_count, nf),
        out_shape=(
            jax.ShapeDtypeStruct((chunks, ndev, ab, LANES), f32),
            jax.ShapeDtypeStruct((own, hb, LANES), f32),
        ),
        in_specs=[hbm] * len(operands),
        out_specs=(hbm,) * 2,
        scratch_shapes=[pltpu.VMEM(x.shape, x.dtype) for x in operands]
        + [
            pltpu.VMEM((chunks, ndev, ab, LANES), f32),
            pltpu.VMEM((chunks, ch_count, seq_count, ab, LANES), f32),
            pltpu.VMEM((ndev, hb, LANES), f32),
            pltpu.VMEM((seq_count, hb, LANES), f32),
            pltpu.VMEM((chunks, ch_count, seq_count, ab, LANES), f32),
            pltpu.VMEM((seq_count, hb, LANES), f32),
            dma((chunks, ndev)), dma((chunks, ndev)), dma((seq_count,)), dma((seq_count,)),
            dma((chunks, ndev)), dma((chunks, ndev)), dma((seq_count,)), dma((own,)),
            dma((len(operands),)), dma((chunks + 1,)),
        ],
        compiler_params=pltpu.CompilerParams(
            collective_id=0, has_side_effects=True, vmem_limit_bytes=VMEM_BYTES
        ),
    )(*operands)
    wide = jax.ShapeDtypeStruct((local_rows, filters), bf16)
    results = (wide, wide, wide, wide, jax.ShapeDtypeStruct((own * nf, local_rows), f32))
    operands = (
        home, tabs[0], query_proj, key_proj, value_proj, grad_mixer,
        skip_gain.reshape(1, filters), filt, sel,
    )
    *outs, grad_filter = pl.pallas_call(
        finish,
        out_shape=results,
        in_specs=[hbm] * len(operands),
        out_specs=(hbm,) * 5,
        scratch_shapes=[pltpu.VMEM(x.shape, x.dtype) for x in operands + results]
        + [dma((len(operands),)), dma((5,))],
        compiler_params=pltpu.CompilerParams(vmem_limit_bytes=VMEM_BYTES),
    )(*operands)
    return (*outs, grad_filter.T)


def solution(mesh):
    in_specs = (
        P("seq", "ch"),
        P("seq", "ch"),
        P("seq", "ch"),
        P("seq", None),
        P("ch"),
        P("seq", "ch"),
    )
    out_specs = (P("seq", "ch"), P("seq", "ch"), P("seq", "ch"), P("seq", "ch"), P("seq", "ch"))
    return jax.shard_map(local, mesh=mesh, in_specs=in_specs, out_specs=out_specs, check_vma=False)
```

time: 43.3 us -> 42 us (0.970)
  Pallas kernels: 42.5 us -> 41.1 us
    pallas_call x1, Pallas kernels: 40 us -> 38.3 us  [local(): pl.pallas_call(functools.partial(kernel, seq_count, ch_count, nf), out_sh...]
where the time goes in v4:
time: 42 us; the launch traced here: 41.8 us
  Pallas kernels  41.1 us (98%)
  between operations  0.64 us (2%)
    pallas_call x1, Pallas kernels, local(): pl.pallas_call(functools.partial(kernel, seq_count, ch_count, nf), out_sh...  38.3 us
    pallas_call x1, Pallas kernels, local(): pl.pallas_call(finish, out_shape=results, in_specs=[hbm] * len(operands),...  2.8 us

profile of v4, /device:TPU:25, one launch (start us, length us, event | category | flops | bytes accessed | tf_op | source)
XLA Modules:
  0.0 41.8 jit_solution(17160868017636776014)
XLA Ops:
  0.6 38.3 %shard_map.191 = (f32[2,32,16,128]{3,2,1,0:T(8,128)}, f32[8,16,128]{2,1,0:T(8,128)}) custom-call(bf16[512,128]{1,0:T(8,128)(2,1)} %refs_2_.3, bf16[512,128]{1,0:T(8,128)(2,1)} %refs_3_.3, bf16[512,128]{1,0:T(8,128)(2,1)} %refs_4_.3, bf16[512,128]{1,0:T(8,128)(2,1)} %refs_5_.2, f32[512,128]{1,0:T(8,128)} %refs_4_.2, ...), custom_call_target="tpu_custom_call" | custom-call | tf_op jit(solution)/shard_map/pallas_call | solution.py:414
  39.0 2.8 %shard_map.192 = (bf16[512,128]{1,0:T(8,128)(2,1)}, bf16[512,128]{1,0:T(8,128)(2,1)}, bf16[512,128]{1,0:T(8,128)(2,1)}, bf16[512,128]{1,0:T(8,128)(2,1)}, f32[32,512]{1,0:T(8,128)}) custom-call(f32[2,32,16,128]{3,2,1,0:T(8,128)} %get-tuple-element.12.refs_0_, bf16[512,512]{1,0:T(8,128)(2,1)} %constant.20.clone.refs_5_.refs_1_, bf16[512,128]{1,0:T(8,128)(2,1)} %refs_2_.3, ...), custom_call_target="tpu_custom_call" | custom-call | tf_op jit(solution)/shard_map/pallas_call | solution.py:444

commit v5 on v4

--- a/solution.py
+++ b/solution.py
@@ -214,6 +214,8 @@
 
     def go(count, at, make):
         def step(i, _):
+            if count % 2 == 0:
+                i = count // 2 + (2 * lax.rem(i, 2) - 1) * (i // 2)
             make(lax.rem(at + i, count)).start()
             return 0
 

time: 42 us -> 42.6 us (1.014)
  the two profiles are of different devices: /device:TPU:25 before, /device:TPU:0 now
where the time goes in v5:
time: 42.6 us; the launch traced here: 42.5 us
  Pallas kernels  41.8 us (98%)
  between operations  0.64 us (2%)
    pallas_call x1, Pallas kernels, local(): pl.pallas_call(functools.partial(kernel, seq_count, ch_count, nf), out_sh...  39 us
    pallas_call x1, Pallas kernels, local(): pl.pallas_call(finish, out_shape=results, in_specs=[hbm] * len(operands),...  2.8 us

profile of v5, /device:TPU:0, one launch (start us, length us, event | category | flops | bytes accessed | tf_op | source)
XLA Modules:
  0.0 42.5 jit_solution(16905943504655541671)
XLA Ops:
  0.6 39.0 %shard_map.191 = (f32[2,32,16,128]{3,2,1,0:T(8,128)}, f32[8,16,128]{2,1,0:T(8,128)}) custom-call(bf16[512,128]{1,0:T(8,128)(2,1)} %refs_2_.3, bf16[512,128]{1,0:T(8,128)(2,1)} %refs_3_.3, bf16[512,128]{1,0:T(8,128)(2,1)} %refs_4_.3, bf16[512,128]{1,0:T(8,128)(2,1)} %refs_5_.2, f32[512,128]{1,0:T(8,128)} %refs_4_.2, ...), custom_call_target="tpu_custom_call" | custom-call | tf_op jit(solution)/shard_map/pallas_call | solution.py:416
  39.7 2.8 %shard_map.192 = (bf16[512,128]{1,0:T(8,128)(2,1)}, bf16[512,128]{1,0:T(8,128)(2,1)}, bf16[512,128]{1,0:T(8,128)(2,1)}, bf16[512,128]{1,0:T(8,128)(2,1)}, f32[32,512]{1,0:T(8,128)}) custom-call(f32[2,32,16,128]{3,2,1,0:T(8,128)} %get-tuple-element.12.refs_0_, bf16[512,512]{1,0:T(8,128)(2,1)} %constant.20.clone.refs_5_.refs_1_, bf16[512,128]{1,0:T(8,128)(2,1)} %refs_2_.3, ...), custom_call_target="tpu_custom_call" | custom-call | tf_op jit(solution)/shard_map/pallas_call | solution.py:446
